TPU v7x, 32 devices: a whole 2x2x4 slice. The times are simulated.
32 devices in a mesh: group: 4 (over z), dom: 8 (over y, x, core).
Axes of the slice: x: 2, y: 2, z: 4, core: 2. Of those that a mesh axis runs over, the one named last changes fastest.
Arguments:
- feats: bfloat16 [4096, 1024], P(('group', 'dom')), may hold values from -6 to 6
- history: bfloat16 [4096, 1024], P(('group', 'dom')), may hold values from -0.25 to 2
- grad_out: bfloat16 [4096, 1024], P(('group', 'dom')), may hold values from -6 to 6
- w_first: bfloat16 [1024, 1024], replicated, may hold values from -0.1875 to 0.1875
- w_second: bfloat16 [1024, 1024], replicated, may hold values from -0.1875 to 0.1875
- send_index: int32 [32, 8, 16], P(('group', 'dom')), may hold values from 0 to 127, as said below
- halo_index: int32 [16384], P(('group', 'dom')), may hold values from 0 to 127
- hub_rows: int32 [32, 32], P(('group', 'dom')), may hold values from 0 to 127
- tile_cols: int32 [32, 4], P(('group', 'dom')), may hold values from 0 to 5
- tile_vals: bfloat16 [32, 4, 128, 128], P(('group', 'dom')), may hold values from -0.25 to 0.25
Outputs:
- new_history: bfloat16 [4096, 1024], P(('group', 'dom'))
- embed_grad: bfloat16 [4096, 1024], P(('group', 'dom'))
- grad_first: float32 [1024, 1024], P(('group', 'dom'))
- grad_second: float32 [1024, 1024], P(('group', 'dom'))
Inputs may be any that keep to these rules, and one draw needn't show every extreme that they name: `send_index`: for each device and each dom peer the 16 rows are distinct. `halo_index`: A value q names slot q % 16 of the rows received from dom peer q // 16 of the same group; values may repeat. `hub_rows`: rows may repeat. `tile_cols`: source tile 0 is the device's own rows, tiles 1 to 4 are halo tiles, tiles 5 and 6 are hub tiles; values may repeat in a row.
All inputs are finite; a program needn't handle non-finite values.
Results may differ from a plain program's by a relative error of at most 0.006.
Values may be sent and summed in bfloat16 or wider, within the bound.
A program may use at most 64 MiB of HBM per device.

v0:
```python
import math

import jax
import jax.numpy as jnp
from jax import lax
from jax.sharding import PartitionSpec as P

D = 1024
V_DEV = 128
TILE = 128
HALO = 512


def combine_tiles(own_rows, halo_rows, hub_panel, tile_cols, tile_vals):
    source = jnp.concatenate([own_rows, halo_rows, hub_panel], axis=0)
    feature_width = source.shape[1]
    picked = source.reshape(-1, tile_vals.shape[2], feature_width)[tile_cols]
    summed = jnp.einsum("rtij,rtjd->rid", tile_vals, picked, preferred_element_type=jnp.float32)
    return summed.reshape(-1, feature_width).astype(jnp.bfloat16)


def reduce_weight(left_rows, right_rows):
    factor = 1.0 / math.sqrt(left_rows.shape[0] * lax.axis_size("group") * lax.axis_size("dom"))
    product = lax.dot_general(
        left_rows, right_rows, (((0,), (0,)), ((), ())), preferred_element_type=jnp.float32
    )
    summed = lax.psum_scatter(product, ("group", "dom"), scatter_dimension=0, tiled=True)
    return summed * factor


def on_device(
    feats,
    history,
    grad_out,
    w_first,
    w_second,
    send_index,
    halo_index,
    hub_rows,
    tile_cols,
    tile_vals,
):
    routes = send_index[0]
    owned_hubs = hub_rows[0]
    feat_slots = lax.all_to_all(feats[routes], "dom", split_axis=0, concat_axis=0, tiled=True)
    feat_halo = feat_slots.reshape(-1, D)[halo_index]
    hub_first = lax.all_gather(feats[owned_hubs], "group", axis=0, tiled=True)
    agg_first = combine_tiles(feats, feat_halo, hub_first, tile_cols, tile_vals)
    z_first = jnp.dot(agg_first, w_first, preferred_element_type=jnp.float32)
    new_history = jax.nn.silu(z_first).astype(jnp.bfloat16)
    hist_slots = lax.all_to_all(history[routes], "dom", split_axis=0, concat_axis=0, tiled=True)
    hist_halo = hist_slots.reshape(-1, D)[halo_index]
    hub_second = lax.all_gather(new_history[owned_hubs], "group", axis=0, tiled=True)
    agg_second = combine_tiles(new_history, hist_halo, hub_second, tile_cols, tile_vals)
    grad_second = reduce_weight(grad_out, agg_second)
    agg_grad = lax.dot_general(
        grad_out, w_second, (((1,), (1,)), ((), ())), preferred_element_type=jnp.float32
    ).astype(jnp.bfloat16)
    source_tiles = (V_DEV + HALO + hub_second.shape[0]) // TILE
    tile_terms = jnp.einsum(
        "rtij,rid->rtjd",
        tile_vals,
        agg_grad.reshape(-1, TILE, D),
        preferred_element_type=jnp.float32,
    )
    selector = (
        tile_cols[:, :, None] == jnp.arange(source_tiles, dtype=jnp.int32)[None, None, :]
    ).astype(jnp.float32)
    spread = jnp.einsum(
        "rts,rtjd->sjd", selector, tile_terms, precision=lax.Precision.HIGHEST
    ).reshape(-1, D)
    own_grad = spread[:V_DEV]
    hub_grad = lax.psum_scatter(spread[V_DEV + HALO :], "group", scatter_dimension=0, tiled=True)
    vertex_grad = own_grad.at[owned_hubs].add(hub_grad)
    gate_value = jax.nn.sigmoid(z_first)
    dz_first = (vertex_grad * gate_value * (1.0 + z_first * (1.0 - gate_value))).astype(
        jnp.bfloat16
    )
    grad_first = reduce_weight(dz_first, agg_first)
    return (new_history, vertex_grad.astype(jnp.bfloat16), grad_first, grad_second)


def solution(mesh):
    placed = (
        P(("group", "dom"), None),
        P(("group", "dom"), None),
        P(("group", "dom"), None),
        P(),
        P(),
        P(("group", "dom"), None, None),
        P(("group", "dom")),
        P(("group", "dom"), None),
        P(("group", "dom"), None),
        P(("group", "dom"), None, None, None),
    )
    return jax.shard_map(
        on_device,
        mesh=mesh,
        in_specs=placed,
        out_specs=(
            P(("group", "dom"), None),
            P(("group", "dom"), None),
            P(("group", "dom"), None),
            P(("group", "dom"), None),
        ),
        check_vma=False,
    )
```

profile of v0, /device:TPU:0, one launch (start us, length us, event | category | flops | bytes accessed | tf_op | source)
XLA Modules:
  0.0 379.5 jit_solution(17820135226478933735)
XLA Ops:
  8.1 2.7 gather_fusion
  10.9 5.2 %all-to-all-start = ((bf16[8,16,1024]{2,1,0:T(8,128)(2,1)}), bf16[8,16,1024]{2,1,0:T(8,128)(2,1)S(1)}, u32[]{:S(2)}, u32[]{:S(2)}) async-start(bf16[8,16,1024]{2,1,0:T(8,128)(2,1)} %bitcast.1), calls=%async_computation | async-start | bytes 524288 | tf_op jit(solution)/shard_map/all_to_all | solution.py:45
  16.1 2.5 fusion.5
  18.6 3.1 copy.22
  21.7 4.3 %fusion = f32[6,128,1024]{2,0,1:T(8,128)S(1)} fusion(f32[1024,4,128]{0,1,2:T(4,128)} %copy.22, s32[4]{0:T(128)S(1)} %bitcast.67), kind=kOutput, calls=%fused_computation.10 | convolution fusion | flops 37748760 | bytes 5242896 | tf_op jit(solution)/shard_map/rts,rtjd->sjd/dot_general | solution.py:69
  26.0 1.6 fusion.18
  29.3 15.8 %all-gather = bf16[128,1024]{1,0:T(8,128)(2,1)S(1)} all-gather(bf16[32,1024]{1,0:T(8,128)(2,1)S(1)} %gather_fusion.2), channel_id=2, replica_groups=mesh['group'=4,'dom'=8] {'group'}, dimensions={0}, use_global_device_ids=true | all-gather | bytes 327680 | tf_op jit(solution)/shard_map/all_gather | solution.py:47
  45.1 1.6 gather_fusion.4
  46.7 3.9 %all-to-all-start.1 = ((bf16[8,16,1024]{2,1,0:T(8,128)(2,1)}), bf16[8,16,1024]{2,1,0:T(8,128)(2,1)S(1)}, u32[]{:S(2)}, u32[]{:S(2)}) async-start(bf16[8,16,1024]{2,1,0:T(8,128)(2,1)} %bitcast.15), calls=%async_computation.3 | async-start | bytes 524288 | tf_op jit(solution)/shard_map/all_to_all | solution.py:51
  50.6 2.8 gather_fusion.1
  53.4 2.5 pad_maximum_fusion
  55.9 3.0 gather_fusion.3
  59.0 1.7 fusion.2
  60.7 3.0 multiply_convert_fusion.1
  64.3 2.8 gather_fusion.5
  67.1 14.0 %all-gather.1 = bf16[128,1024]{1,0:T(8,128)(2,1)S(1)} all-gather(bf16[32,1024]{1,0:T(8,128)(2,1)S(1)} %gather_fusion.6), channel_id=3, replica_groups=mesh['group'=4,'dom'=8] {'group'}, dimensions={0}, use_global_device_ids=true | all-gather | bytes 327680 | tf_op jit(solution)/shard_map/all_gather | solution.py:53
  81.1 2.5 pad_maximum_fusion.1
  83.7 2.1 gather_fusion.7
  85.7 3.4 convolution_bitcast_fusion
  91.8 3.8 fusion.6
  96.3 135.8 %reduce-scatter.8.cloned.1.call-done = f32[32,1024]{1,0:T(8,128)} async-done(((f32[1024,1024]{1,0:T(8,128)}), f32[32,1024]{1,0:T(8,128)}) %reduce-scatter.8.cloned.1.call-update) | async-done | bytes 131088 | tf_op jit(solution)/shard_map/reduce_scatter | solution.py:27
  232.2 1.6 broadcast_multiply_fusion
  233.8 137.6 %reduce-scatter.6.cloned.1.call-done = f32[32,1024]{1,0:T(8,128)} async-done(((f32[1024,1024]{1,0:T(8,128)}), f32[32,1024]{1,0:T(8,128)}) %reduce-scatter.6.cloned.1.call-update) | async-done | bytes 131088 | tf_op jit(solution)/shard_map/reduce_scatter | solution.py:27
  371.4 1.6 broadcast_multiply_fusion.1
  (50 shorter events, 6.6 us)
Async XLA Ops:
  7.2 8.9 %copy-start = (bf16[1024,1024]{1,0:T(8,128)(2,1)S(1)}, bf16[1024,1024]{1,0:T(8,128)(2,1)}, u32[]{:S(2)}) copy-start(bf16[1024,1024]{1,0:T(8,128)(2,1)} %param.14) | copy-start | bytes 6291460
  7.2 8.9 %copy-start.5 = (bf16[1,4,128,128]{3,2,1,0:T(8,128)(2,1)S(1)}, bf16[1,4,128,128]{3,2,1,0:T(8,128)(2,1)}, u32[]{:S(2)}) copy-start(bf16[1,4,128,128]{3,2,1,0:T(8,128)(2,1)} %param.19) | copy-start | bytes 393220
  7.2 8.9 %copy-start.6 = (bf16[128,1024]{1,0:T(8,128)(2,1)S(1)}, bf16[128,1024]{1,0:T(8,128)(2,1)}, u32[]{:S(2)}) copy-start(bf16[128,1024]{1,0:T(8,128)(2,1)} %param.12) | copy-start | bytes 786436
  10.9 35.8 %all-to-all-start = ((bf16[8,16,1024]{2,1,0:T(8,128)(2,1)}), bf16[8,16,1024]{2,1,0:T(8,128)(2,1)S(1)}, u32[]{:S(2)}, u32[]{:S(2)}) async-start(bf16[8,16,1024]{2,1,0:T(8,128)(2,1)} %bitcast.1), calls=%async_computation | async-start | bytes 524288 | tf_op jit(solution)/shard_map/all_to_all | solution.py:45
  16.0 74.3 %reduce-scatter.4.cloned.1.call-start = ((), (), s32[]{:S(2)}) async-start(), calls=%async_computation.5 | async-start | bytes 655360 | tf_op jit(solution)/shard_map/reduce_scatter | solution.py:73
  18.6 3.1 copy-start.11
  26.0 2.6 copy-start.12
  26.0 2.6 copy-start.1
  26.0 3.2 copy-start.10
  26.0 19.1 %copy-start.2 = (bf16[128,1024]{1,0:T(8,128)(2,1)S(1)}, bf16[128,1024]{1,0:T(8,128)(2,1)}, u32[]{:S(2)}) copy-start(bf16[128,1024]{1,0:T(8,128)(2,1)} %param.11) | copy-start | bytes 786436
  46.7 17.6 %all-to-all-start.1 = ((bf16[8,16,1024]{2,1,0:T(8,128)(2,1)}), bf16[8,16,1024]{2,1,0:T(8,128)(2,1)S(1)}, u32[]{:S(2)}, u32[]{:S(2)}) async-start(bf16[8,16,1024]{2,1,0:T(8,128)(2,1)} %bitcast.15), calls=%async_computation.3 | async-start | bytes 524288 | tf_op jit(solution)/shard_map/all_to_all | solution.py:51
  50.6 181.6 %reduce-scatter.8.cloned.1.call-start = ((), (), s32[]{:S(2)}) async-start(), calls=%async_computation.7 | async-start | bytes 4325376 | tf_op jit(solution)/shard_map/reduce_scatter | solution.py:27
  60.7 3.6 copy-start.8
  63.7 17.5 %copy-start.3 = (bf16[128,1024]{1,0:T(8,128)(2,1)}, bf16[128,1024]{1,0:T(8,128)(2,1)S(1)}, u32[]{:S(2)}) copy-start(bf16[128,1024]{1,0:T(8,128)(2,1)S(1)} %get-tuple-element.6) | copy-start | bytes 786436
  83.7 2.1 copy-start.7
  89.2 1.0 copy-start.4
  89.2 2.6 copy-start.9
  89.2 282.2 %reduce-scatter.6.cloned.1.call-start = ((), (), s32[]{:S(2)}) async-start(), calls=%async_computation.6 | async-start | bytes 4325376 | tf_op jit(solution)/shard_map/reduce_scatter | solution.py:27
Sparse Core Ops, SparseCore 0:
  28.7 25.1 reduce-scatter.3
  89.3 142.8 reduce-scatter.7
  234.5 136.8 reduce-scatter.5
where the time goes:
time: 380 us; the launch traced here: 379 us
  waiting for transfers between devices  274 us (72%)
  blocking collectives  29.8 us (8%)
  local copies, waits for them, and re-layouts  23.1 us (6%)
  matrix products  18.7 us (5%)
  between operations  14 us (4%)
  other arithmetic  11.2 us (3%)
  starting transfers between devices  9.15 us (2%)
    reduce_scatter x2, waiting for transfers between devices, reduce_weight(): lax.psum_scatter(product, ('group', 'dom'), scatter_dimension=0, tiled=True)  273 us
    all_gather x1, blocking collectives, on_device(): hub_first = lax.all_gather(feats[owned_hubs], 'group', axis=0, tiled=True)  15.8 us
    all_gather x1, blocking collectives, on_device(): lax.all_gather(new_history[owned_hubs], 'group', axis=0, tiled=True)  14 us
  transfers between devices with their start and end apart: 5, of which 2 were waited for; matrix products, arithmetic and copies ran while one was open for 12% of the time, Pallas kernels for 0%

commit v1 on v0

--- a/solution.py
+++ b/solution.py
@@ -20,11 +20,16 @@
 
 
 def reduce_weight(left_rows, right_rows):
-    factor = 1.0 / math.sqrt(left_rows.shape[0] * lax.axis_size("group") * lax.axis_size("dom"))
+    groups, doms = lax.axis_size("group"), lax.axis_size("dom")
+    factor = 1.0 / math.sqrt(left_rows.shape[0] * groups * doms)
+    rows = left_rows.shape[0]
+    gathered = lax.all_gather(right_rows, "dom", axis=0, tiled=True)
+    by_dom = left_rows.reshape(rows, groups, doms, -1).transpose(2, 0, 1, 3).reshape(doms * rows, -1)
+    columns = lax.all_to_all(by_dom, "dom", split_axis=0, concat_axis=0, tiled=True)
     product = lax.dot_general(
-        left_rows, right_rows, (((0,), (0,)), ((), ())), preferred_element_type=jnp.float32
+        columns, gathered, (((0,), (0,)), ((), ())), preferred_element_type=jnp.float32
     )
-    summed = lax.psum_scatter(product, ("group", "dom"), scatter_dimension=0, tiled=True)
+    summed = lax.psum_scatter(product, "group", scatter_dimension=0, tiled=True)
     return summed * factor
 
 

time: 380 us -> 163 us (0.43)
  waiting for transfers between devices: 274 us -> 32.7 us
  blocking collectives: 29.8 us -> 52 us
    reduce_scatter x2, waiting for transfers between devices: 273 us -> 21.8 us  [reduce_weight(): summed = lax.psum_scatter(product, 'group', scatter_dimension=0, tiled=True)]
    all_to_all x0 -> x2, blocking collectives: none -> 21.6 us  [reduce_weight(): lax.all_to_all(by_dom, 'dom', split_axis=0, concat_axis=0, tiled=True)]
    all_to_all x1, waiting for transfers between devices: 0.01 us -> 7.28 us  [on_device(): lax.all_to_all(history[routes], 'dom', split_axis=0, concat_axis=0, tiled...]
  transfers between devices with their start and end apart: 5 -> 7, of which waited for: 2 -> 4; matrix products, arithmetic and copies ran while one was open for 12% -> 22% of each run, Pallas kernels for 0% -> 0%
where the time goes in v1:
time: 163 us; the launch traced here: 162 us
  blocking collectives  52 us (32%)
  waiting for transfers between devices  32.7 us (20%)
  local copies, waits for them, and re-layouts  23 us (14%)
  matrix products  19.6 us (12%)
  between operations  15.5 us (10%)
  other arithmetic  9.65 us (6%)
  starting transfers between devices  9.18 us (6%)
    reduce_scatter x2, waiting for transfers between devices, reduce_weight(): summed = lax.psum_scatter(product, 'group', scatter_dimension=0, tiled=True)  21.8 us
    all_to_all x2, blocking collectives, reduce_weight(): lax.all_to_all(by_dom, 'dom', split_axis=0, concat_axis=0, tiled=True)  21.6 us
    all_gather x1, blocking collectives, on_device(): hub_first = lax.all_gather(feats[owned_hubs], 'group', axis=0, tiled=True)  16.4 us
    all_gather x1, blocking collectives, on_device(): lax.all_gather(new_history[owned_hubs], 'group', axis=0, tiled=True)  14 us
    all_to_all x1, waiting for transfers between devices, on_device(): lax.all_to_all(history[routes], 'dom', split_axis=0, concat_axis=0, tiled...  7.28 us
    dot_general x2, matrix products, reduce_weight(): lax.dot_general(columns, gathered, (((0,), (0,)), ((), ())), preferred_el...  6.44 us
    all_to_all x1, starting transfers between devices, on_device(): lax.all_to_all(feats[routes], 'dom', split_axis=0, concat_axis=0, tiled=T...  5.17 us
    concatenate x2, other arithmetic, combine_tiles(): source = jnp.concatenate([own_rows, halo_rows, hub_panel], axis=0)  5.03 us
  transfers between devices with their start and end apart: 7, of which 4 were waited for; matrix products, arithmetic and copies ran while one was open for 22% of the time, Pallas kernels for 0%

profile of v1, /device:TPU:0, one launch (start us, length us, event | category | flops | bytes accessed | tf_op | source)
XLA Modules:
  0.0 161.7 jit_solution(16511951574302812723)
XLA Ops:
  9.6 3.5 %convolution_bitcast_fusion = f32[4,128,1024]{1,2,0:T(8,128)} fusion(bf16[128,1024]{1,0:T(8,128)(2,1)} %param.12, bf16[1024,1024]{1,0:T(8,128)(2,1)S(1)} %copy-done, bf16[1,4,128,128]{3,2,1,0:T(8,128)(2,1)} %param.19), kind=kOutput, calls=%fused_computation.9 | convolution fusion | flops 402784256 | bytes 4587520 | tf_op jit(solution)/shard_map/rtij,rid->rtjd/dot_general | solution.py:65
  13.1 3.1 %copy.39 = f32[4,128,1024]{2,0,1:T(4,128)} copy(f32[4,128,1024]{1,2,0:T(8,128)} %convolution_bitcast_fusion) | data formatting | bytes 4194304 | tf_op jit(solution)/shard_map/rtij,rid->rtjd/dot_general | solution.py:65
  16.1 4.3 %fusion.8 = f32[6,128,1024]{2,0,1:T(8,128)S(1)} fusion(f32[4,128,1024]{2,0,1:T(4,128)} %copy.39, s32[4]{0:T(128)S(1)} %bitcast.88), kind=kOutput, calls=%fused_computation.40 | convolution fusion | flops 37748760 | bytes 5242896 | tf_op jit(solution)/shard_map/rts,rtjd->sjd/dot_general | solution.py:74
  20.5 1.6 fusion.13
  24.6 5.2 %all-to-all-start = ((bf16[8,16,1024]{2,1,0:T(8,128)(2,1)}), bf16[8,16,1024]{2,1,0:T(8,128)(2,1)S(1)}, u32[]{:S(2)}, u32[]{:S(2)}) async-start(bf16[8,16,1024]{2,1,0:T(8,128)(2,1)} %bitcast.1), calls=%async_computation | async-start | bytes 524288 | tf_op jit(solution)/shard_map/all_to_all | solution.py:50
  30.6 16.4 %all-gather = bf16[128,1024]{1,0:T(8,128)(2,1)S(1)} all-gather(bf16[32,1024]{1,0:T(8,128)(2,1)S(1)} %gather_fusion.2), channel_id=2, replica_groups=mesh['group'=4,'dom'=8] {'group'}, dimensions={0}, use_global_device_ids=true | all-gather | bytes 327680 | tf_op jit(solution)/shard_map/all_gather | solution.py:52
  47.0 2.8 %gather_fusion.1 = bf16[512,1024]{1,0:T(8,128)(2,1)} fusion(bf16[128,1024]{1,0:T(8,128)(2,1)S(1)} %bitcast.75, s32[1024]{0:T(1024)S(1)} %pad_clamp_fusion.2), kind=kCustom, calls=%fused_computation.1 | custom fusion | bytes 2099200 | tf_op jit(solution)/shard_map/gather | solution.py:51
  49.8 2.5 %pad_maximum_fusion = bf16[768,1024]{1,0:T(8,128)(2,1)} fusion(bf16[128,1024]{1,0:T(8,128)(2,1)S(1)} %all-gather, bf16[512,1024]{1,0:T(8,128)(2,1)} %gather_fusion.1, bf16[128,1024]{1,0:T(8,128)(2,1)S(1)} %copy-done.1), kind=kLoop, calls=%fused_computation.10 | loop fusion | flops 4718592 | bytes 3145728 | tf_op jit(solution)/shard_map/concatenate | solution.py:15
  52.3 2.1 %gather_fusion.3 = bf16[4,128,1024]{2,1,0:T(8,128)(2,1)S(1)} fusion(bf16[6,128,1024]{2,1,0:T(8,128)(2,1)} %bitcast.79, s32[1024]{0:T(1024)S(1)} %pad_clamp_fusion), kind=kCustom, calls=%fused_computation.3 | custom fusion | bytes 2097168 | tf_op jit(solution)/shard_map/gather | solution.py:17
  57.2 3.8 %all-to-all-start.2 = ((bf16[8,16,1024]{2,1,0:T(8,128)(2,1)}), bf16[8,16,1024]{2,1,0:T(8,128)(2,1)S(1)}, u32[]{:S(2)}, u32[]{:S(2)}) async-start(bf16[8,16,1024]{2,1,0:T(8,128)(2,1)} %bitcast.20), calls=%async_computation.4 | async-start | bytes 524288 | tf_op jit(solution)/shard_map/all_to_all | solution.py:56
  61.2 7.3 %all-to-all-done.2 = bf16[8,16,1024]{2,1,0:T(8,128)(2,1)S(1)} async-done(((bf16[8,16,1024]{2,1,0:T(8,128)(2,1)}), bf16[8,16,1024]{2,1,0:T(8,128)(2,1)S(1)}, u32[]{:S(2)}, u32[]{:S(2)}) %all-to-all-start.2) | async-done | bytes 262176 | tf_op jit(solution)/shard_map/all_to_all | solution.py:56
  68.4 2.8 %gather_fusion.5 = bf16[512,1024]{1,0:T(8,128)(2,1)} fusion(bf16[128,1024]{1,0:T(8,128)(2,1)S(1)} %bitcast.76, s32[1024]{0:T(1024)S(1)} %pad_clamp_fusion.2), kind=kCustom, calls=%fused_computation.5 | custom fusion | bytes 2099200 | tf_op jit(solution)/shard_map/gather | solution.py:57
  72.7 3.0 %multiply_convert_fusion = (bf16[128,1024]{1,0:T(8,128)(2,1)}, bf16[128,1024]{1,0:T(8,128)(2,1)}, bf16[128,1024]{1,0:T(8,128)(2,1)S(1)}) fusion(f32[128,1024]{1,0:T(8,128)S(1)} %scatter_fusion, bf16[1024,128]{1,0:T(8,128)(2,1)S(1)} %copy-done.7, bf16[1024,1024]{1,0:T(8,128)(2,1)} %param.13), kind=kOutput, calls=%fused_computation.22 | convolution fusion | flops 270008320 | bytes 3670016 | tf_op jit(solution)/shard_map/dot_general | solution.py:54
  76.3 14.0 %all-gather.1 = bf16[128,1024]{1,0:T(8,128)(2,1)S(1)} all-gather(bf16[32,1024]{1,0:T(8,128)(2,1)S(1)} %gather_fusion.6), channel_id=3, replica_groups=mesh['group'=4,'dom'=8] {'group'}, dimensions={0}, use_global_device_ids=true | all-gather | bytes 327680 | tf_op jit(solution)/shard_map/all_gather | solution.py:58
  90.3 2.5 %pad_maximum_fusion.1 = bf16[768,1024]{1,0:T(8,128)(2,1)} fusion(bf16[128,1024]{1,0:T(8,128)(2,1)S(1)} %all-gather.1, bf16[512,1024]{1,0:T(8,128)(2,1)} %gather_fusion.5, bf16[128,1024]{1,0:T(8,128)(2,1)S(1)} %get-tuple-element.8), kind=kLoop, calls=%fused_computation.11 | loop fusion | flops 4718592 | bytes 3145728 | tf_op jit(solution)/shard_map/concatenate | solution.py:15
  92.8 2.0 %gather_fusion.7 = bf16[4,128,1024]{2,1,0:T(8,128)(2,1)S(1)} fusion(bf16[6,128,1024]{2,1,0:T(8,128)(2,1)} %bitcast.78, s32[1024]{0:T(1024)S(1)} %pad_clamp_fusion), kind=kCustom, calls=%fused_computation.7 | custom fusion | bytes 2097168 | tf_op jit(solution)/shard_map/gather | solution.py:17
  97.3 9.5 %all_to_all.34 = bf16[8,128,128]{1,2,0:T(8,128)(2,1)S(1)} all-to-all(bf16[8,128,128]{1,2,0:T(8,128)(2,1)S(1)} %bitcast.82), channel_id=1, replica_groups=mesh['group'=4,'dom'=8] {'dom'}, dimensions={0} | all-to-all | bytes 524288 | tf_op jit(solution)/shard_map/all_to_all | solution.py:28
  107.0 3.2 %fusion.14 = f32[128,1024]{1,0:T(8,128)} fusion(bf16[1024,128]{1,0:T(8,128)(2,1)S(1)} %bitcast.86, bf16[1024,1024]{0,1:T(8,128)(2,1)} %all-gather.5.cloned.1.call-done), kind=kOutput, calls=%fused_computation.45 | convolution fusion | flops 268435456 | bytes 2883584 | tf_op jit(solution)/shard_map/dot_general | solution.py:29
  110.5 12.2 %all_to_all.35 = bf16[8,128,128]{1,2,0:T(8,128)(2,1)S(1)} all-to-all(bf16[8,128,128]{1,2,0:T(8,128)(2,1)S(1)} %bitcast.83), channel_id=1, replica_groups=mesh['group'=4,'dom'=8] {'dom'}, dimensions={0} | all-to-all | bytes 524288 | tf_op jit(solution)/shard_map/all_to_all | solution.py:28
  122.8 3.6 %all-gather.7.cloned.1.call-done = bf16[1024,1024]{0,1:T(8,128)(2,1)} async-done(((bf16[128,1024]{0,1:T(8,128)(2,1)}), bf16[1024,1024]{0,1:T(8,128)(2,1)}) %all-gather.7.cloned.1.call-update) | async-done | bytes 2097168 | tf_op jit(solution)/shard_map/all_gather | solution.py:26
  126.4 3.2 %convolution_bitcast_fusion.1 = f32[128,1024]{1,0:T(8,128)} fusion(bf16[1024,1024]{0,1:T(8,128)(2,1)} %all-gather.7.cloned.1.call-done, bf16[1024,128]{1,0:T(8,128)(2,1)S(1)} %bitcast.87), kind=kOutput, calls=%fused_computation.12 | convolution fusion | flops 268435456 | bytes 2883584 | tf_op jit(solution)/shard_map/dot_general | solution.py:29
  130.7 1.6 broadcast_multiply_fusion.1
  132.3 20.7 %reduce-scatter.8.cloned.1.call-done = f32[32,1024]{1,0:T(8,128)} async-done(((f32[128,1024]{1,0:T(8,128)}), f32[32,1024]{1,0:T(8,128)}) %reduce-scatter.8.cloned.1.call-update) | async-done | bytes 131088 | tf_op jit(solution)/shard_map/reduce_scatter | solution.py:32
  153.0 1.6 broadcast_multiply_fusion
  (66 shorter events, 14.0 us)
Async XLA Ops:
  8.0 1.6 copy-start
  8.0 63.2 %reduce-scatter.4.cloned.1.call-start = ((), (), s32[]{:S(2)}) async-start(), calls=%async_computation.7 | async-start | bytes 655360 | tf_op jit(solution)/shard_map/reduce_scatter | solution.py:78
  13.0 3.1 %copy-start.12 = (s32[1,4]{1,0:T(1,128)S(1)}, s32[1,4]{1,0:T(1,128)}, u32[]{:S(2)}) copy-start(s32[1,4]{1,0:T(1,128)} %param.18) | copy-start | bytes 52
  20.4 2.5 %copy-start.8 = (s32[1,8,16]{2,1,0:T(8,128)S(1)}, s32[1,8,16]{2,1,0:T(8,128)}, u32[]{:S(2)}) copy-start(s32[1,8,16]{2,1,0:T(8,128)} %param.15) | copy-start | bytes 1540
  20.4 2.6 %copy-start.1 = (bf16[128,1024]{1,0:T(8,128)(2,1)S(1)}, bf16[128,1024]{1,0:T(8,128)(2,1)}, u32[]{:S(2)}) copy-start(bf16[128,1024]{1,0:T(8,128)(2,1)} %param.10) | copy-start | bytes 786436
  22.0 7.8 %copy-start.13 = (s32[1,32]{1,0:T(1,128)S(1)}, s32[1,32]{1,0:T(1,128)}, u32[]{:S(2)}) copy-start(s32[1,32]{1,0:T(1,128)} %param.17) | copy-start | bytes 388
  22.9 7.6 %copy-start.11 = (s32[512]{0:T(512)S(1)}, s32[512]{0:T(512)}, u32[]{:S(2)}) copy-start(s32[512]{0:T(512)} %param.16) | copy-start | bytes 6148
  24.6 22.4 %all-to-all-start = ((bf16[8,16,1024]{2,1,0:T(8,128)(2,1)}), bf16[8,16,1024]{2,1,0:T(8,128)(2,1)S(1)}, u32[]{:S(2)}, u32[]{:S(2)}) async-start(bf16[8,16,1024]{2,1,0:T(8,128)(2,1)} %bitcast.1), calls=%async_computation | async-start | bytes 524288 | tf_op jit(solution)/shard_map/all_to_all | solution.py:50
  29.8 77.2 %all-gather.5.cloned.1.call-start = ((), (), s32[]{:S(2)}) async-start(), calls=%async_computation.8 | async-start | bytes 2359296 | tf_op jit(solution)/shard_map/all_gather | solution.py:26
  29.9 0.7 copy-start.9
  49.8 4.6 %copy-start.5 = (bf16[1,4,128,128]{3,2,1,0:T(8,128)(2,1)S(1)}, bf16[1,4,128,128]{3,2,1,0:T(8,128)(2,1)}, u32[]{:S(2)}) copy-start(bf16[1,4,128,128]{3,2,1,0:T(8,128)(2,1)} %param.19) | copy-start | bytes 393220
  52.3 3.3 %copy-start.2 = (bf16[128,1024]{1,0:T(8,128)(2,1)S(1)}, bf16[128,1024]{1,0:T(8,128)(2,1)}, u32[]{:S(2)}) copy-start(bf16[128,1024]{1,0:T(8,128)(2,1)} %param.11) | copy-start | bytes 786436
  55.6 5.5 %copy-start.4 = (f32[1,128,1024]{2,0,1:T(1,128)S(1)}, f32[1,128,1024]{2,0,1:T(1,128)}, u32[]{:S(2)}) copy-start(f32[1,128,1024]{2,0,1:T(1,128)} %get-tuple-element.5) | copy-start | bytes 1572868
  57.2 11.3 %all-to-all-start.2 = ((bf16[8,16,1024]{2,1,0:T(8,128)(2,1)}), bf16[8,16,1024]{2,1,0:T(8,128)(2,1)S(1)}, u32[]{:S(2)}, u32[]{:S(2)}) async-start(bf16[8,16,1024]{2,1,0:T(8,128)(2,1)} %bitcast.20), calls=%async_computation.4 | async-start | bytes 524288 | tf_op jit(solution)/shard_map/all_to_all | solution.py:56
  61.0 65.4 %all-gather.7.cloned.1.call-start = ((), (), s32[]{:S(2)}) async-start(), calls=%async_computation.10 | async-start | bytes 2359296 | tf_op jit(solution)/shard_map/all_gather | solution.py:26
  68.4 2.8 %copy-start.10 = (s32[32]{0:T(128)S(1)}, s32[32]{0:T(128)}, u32[]{:S(2)}) copy-start(s32[32]{0:T(128)} %copy-done.9) | copy-start | bytes 388
  71.2 1.5 copy-start.7
  75.7 19.1 %copy-start.3 = (bf16[128,1024]{1,0:T(8,128)(2,1)}, bf16[128,1024]{1,0:T(8,128)(2,1)S(1)}, u32[]{:S(2)}) copy-start(bf16[128,1024]{1,0:T(8,128)(2,1)S(1)} %get-tuple-element.8) | copy-start | bytes 786436
  96.1 34.6 %reduce-scatter.6.cloned.1.call-start = ((), (), s32[]{:S(2)}) async-start(), calls=%async_computation.9 | async-start | bytes 655360 | tf_op jit(solution)/shard_map/reduce_scatter | solution.py:32
  106.8 3.5 %copy-start.6 = (bf16[128,1024]{1,0:T(8,128)(2,1)S(1)}, bf16[128,1024]{1,0:T(8,128)(2,1)}, u32[]{:S(2)}) copy-start(bf16[128,1024]{1,0:T(8,128)(2,1)} %param.12) | copy-start | bytes 786436
  110.2 42.8 %reduce-scatter.8.cloned.1.call-start = ((), (), s32[]{:S(2)}) async-start(), calls=%async_computation.11 | async-start | bytes 655360 | tf_op jit(solution)/shard_map/reduce_scatter | solution.py:32
Sparse Core Ops, SparseCore 0:
  23.1 25.8 reduce-scatter.3
  110.3 20.3 reduce-scatter.5
  133.0 19.9 reduce-scatter.7
Sparse Core Ops, SparseCore 1:
  55.7 29.1 all-gather.4
  96.2 30.2 all-gather.6

commit v2 on v1

--- a/solution.py
+++ b/solution.py
@@ -1,8 +1,11 @@
+import functools
 import math
 
 import jax
 import jax.numpy as jnp
 from jax import lax
+from jax.experimental import pallas as pl
+from jax.experimental.pallas import tpu as pltpu
 from jax.sharding import PartitionSpec as P
 
 D = 1024
@@ -85,6 +88,360 @@
     return (new_history, vertex_grad.astype(jnp.bfloat16), grad_first, grad_second)
 
 
+BF16, F32 = jnp.bfloat16, jnp.float32
+
+
+def dot(left, right, contract=(1, 0)):
+    dims = (((contract[0],), (contract[1],)), ((), ()))
+    return lax.dot_general(left, right, dims, preferred_element_type=F32)
+
+
+def halves(weights):
+    high = weights.astype(BF16)
+    low = (weights - high.astype(F32)).astype(BF16)
+    return jnp.concatenate([high, low], axis=0)
+
+
+def apply_halves(pair, rows):
+    both = dot(pair, rows)
+    count = pair.shape[0] // 2
+    return both[:count] + both[count:]
+
+
+def window_kernel(
+    groups,
+    doms,
+    feats,
+    history,
+    grad_out,
+    index_rows,
+    tile_cols,
+    tile_vals,
+    w_first,
+    w_second,
+    new_history,
+    embed_grad,
+    grad_first,
+    grad_second,
+    w_first_held,
+    w_second_held,
+    send_feats,
+    send_hist,
+    send_hubs,
+    send_fresh,
+    slots_feats,
+    slots_hist,
+    hubs_first,
+    hubs_second,
+    all_grad_out,
+    all_agg,
+    hub_terms,
+    hub_arrived,
+    own_grad,
+    gate_slope,
+    dz_out,
+    dz_in,
+    agg_out,
+    agg_in,
+    first_terms,
+    first_sent,
+    first_in,
+    second_terms,
+    second_sent,
+    second_in,
+    rows_out,
+    rows_in,
+    local_sems,
+    send_sems,
+    recv_sems,
+):
+    group, dom = lax.axis_index("group"), lax.axis_index("dom")
+    chips = doms // 2
+    chip, core = dom // 2, dom % 2
+    factor = 1.0 / math.sqrt(V_DEV * groups * doms)
+    share = D // (groups * doms)
+    dom_peers = [(dom + off) % doms for off in range(1, doms)]
+    group_peers = [(group + off) % groups for off in range(1, groups)]
+    sibling = dom + 1 - 2 * core
+    chip_peers = [((chip + off) % chips) * 2 + core for off in range(1, chips)]
+    chip_sources = [((chip + chips - off) % chips) * 2 + core for off in range(1, chips)]
+    used = []
+
+    load_second = pltpu.make_async_copy(w_second, w_second_held, local_sems.at[0])
+    load_second.start()
+    load_first = pltpu.make_async_copy(w_first, w_first_held, local_sems.at[1])
+    load_first.start()
+
+    barrier = pltpu.get_barrier_semaphore()
+    for peer in dom_peers:
+        pl.semaphore_signal(
+            barrier, inc=1, device_id=(group, peer), device_id_type=pl.DeviceIdType.MESH
+        )
+    for peer in group_peers:
+        pl.semaphore_signal(
+            barrier, inc=1, device_id=(peer, dom), device_id_type=pl.DeviceIdType.MESH
+        )
+
+    def send(source, target, to_group, to_dom):
+        copy = pltpu.make_async_remote_copy(
+            src_ref=source,
+            dst_ref=target,
+            send_sem=send_sems.at[len(used)],
+            recv_sem=recv_sems.at[len(used)],
+            device_id=(to_group, to_dom),
+            device_id_type=pl.DeviceIdType.MESH,
+        )
+        used.append(copy)
+        copy.start()
+        return copy
+
+    def to_doms(source, target):
+        return [send(source.at[peer], target.at[dom], group, peer) for peer in dom_peers]
+
+    def to_groups(source, target):
+        return [send(source.at[peer], target.at[group], peer, dom) for peer in group_peers]
+
+    def share_to_groups(source, target):
+        return [send(source, target.at[group], peer, dom) for peer in group_peers]
+
+    def to_chips(source, target):
+        near = send(source, target.at[dom], group, sibling)
+        return near, [send(source, target.at[dom], group, peer) for peer in chip_peers]
+
+    def forward(far, target):
+        passed = []
+        for copy, origin in zip(far, chip_sources):
+            copy.wait_recv()
+            passed.append(send(target.at[origin], target.at[origin], group, sibling))
+        return passed
+
+    def arrived(copies):
+        for copy in copies:
+            copy.wait_recv()
+
+    sublane = lax.broadcasted_iota(jnp.int32, (V_DEV, V_DEV), 0)
+    lane_row = lax.broadcasted_iota(jnp.int32, (1, V_DEV), 1)
+    route_cols = (sublane == index_rows[0:1, :]).astype(F32)
+    hub_cols = (sublane == index_rows[1:2, :]).astype(F32)
+    route_pick = route_cols.T.astype(BF16)
+    hub_count = V_DEV // groups
+    hub_pick = hub_cols.T[:hub_count].astype(BF16)
+    hub_spread = hub_cols.astype(BF16)
+
+    send_feats[...] = dot(route_pick, feats[...]).astype(BF16).reshape(send_feats.shape)
+    send_hubs[...] = dot(hub_pick, feats[...]).astype(BF16)
+    pl.semaphore_wait(barrier, doms - 1 + groups - 1)
+    feat_copies = to_doms(send_feats, slots_feats)
+    hub_copies = share_to_groups(send_hubs, hubs_first)
+    slots_feats[dom] = send_feats[dom]
+    hubs_first[group] = send_hubs[...]
+    send_hist[...] = dot(route_pick, history[...]).astype(BF16).reshape(send_hist.shape)
+    hist_copies = to_doms(send_hist, slots_hist)
+    slots_hist[dom] = send_hist[dom]
+    grad_near, grad_far = to_chips(grad_out, all_grad_out)
+    all_grad_out[dom] = grad_out[...]
+
+    places = 3 * V_DEV
+    place_of = lax.broadcasted_iota(jnp.int32, (places, V_DEV), 0)
+    weights = jnp.zeros((V_DEV, places), F32)
+    halo_tiles = HALO // TILE
+    for tile in range(tile_vals.shape[1]):
+        column = tile_cols[0:1, tile : tile + 1]
+        target = jnp.where(column == 0, lane_row, lane_row + 2 * V_DEV)
+        for halo in range(halo_tiles):
+            slot = index_rows[2 + halo : 3 + halo, :] + V_DEV
+            target = jnp.where(column == halo + 1, slot, target)
+        chosen = (place_of == target).astype(F32).astype(BF16)
+        weights = weights + dot(tile_vals[0, tile], chosen, (1, 1))
+    own, slot, hub = (weights[:, n * V_DEV : (n + 1) * V_DEV] for n in range(3))
+    own_pair, slot_pair, hub_pair = halves(own), halves(slot), halves(hub)
+
+    load_second.wait()
+    agg_grad = dot(grad_out[...], w_second_held[...], (1, 1)).astype(BF16)
+    hub_terms[...] = apply_halves(halves(hub.T), agg_grad).astype(BF16).reshape(hub_terms.shape)
+    term_copies = to_groups(hub_terms, hub_arrived)
+    hub_arrived[group] = hub_terms[group]
+    own_grad[...] = apply_halves(halves(own.T), agg_grad)
+
+    first = apply_halves(own_pair, feats[...])
+    arrived(feat_copies)
+    first = first + apply_halves(slot_pair, slots_feats[...].reshape(V_DEV, D))
+    arrived(hub_copies)
+    first = first + apply_halves(hub_pair, hubs_first[...].reshape(V_DEV, D))
+    agg_first = first.astype(BF16)
+    all_agg[dom] = agg_first
+    agg_near, agg_far = to_chips(all_agg.at[dom], all_agg)
+
+    load_first.wait()
+    z_first = dot(agg_first, w_first_held[...])
+    gate = 1.0 / (1.0 + jnp.exp(-z_first))
+    fresh = (z_first * gate).astype(BF16)
+    new_history[...] = fresh
+    send_fresh[...] = dot(hub_pick, fresh).astype(BF16)
+    fresh_copies = share_to_groups(send_fresh, hubs_second)
+    hubs_second[group] = send_fresh[...]
+    gate_slope[...] = gate * (1.0 + z_first * (1.0 - gate))
+
+    arrived(term_copies)
+    vertex_grad = own_grad[...] + dot(hub_spread, hub_arrived[...].reshape(V_DEV, D))
+    embed_grad[...] = vertex_grad.astype(BF16)
+    own_grad[...] = vertex_grad * gate_slope[...]
+    for g in range(groups):
+        for d in range(0, doms * share, TILE):
+            start = g * doms * share + d
+            block = own_grad[:, start : start + TILE].T.astype(BF16)
+            for piece in range(TILE // share):
+                dz_out[d // share + piece, g * share : (g + 1) * share, :] = block[
+                    piece * share : (piece + 1) * share
+                ]
+    dz_copies = to_doms(dz_out, dz_in)
+    dz_in[dom] = dz_out[dom]
+
+    arrived(hist_copies)
+    second = apply_halves(own_pair, new_history[...])
+    second = second + apply_halves(slot_pair, slots_hist[...].reshape(V_DEV, D))
+    arrived(fresh_copies)
+    second = second + apply_halves(hub_pair, hubs_second[...].reshape(V_DEV, D))
+    wide = D // doms
+    for d in range(doms):
+        agg_out[d] = second[:, d * wide : (d + 1) * wide].T.astype(BF16)
+    agg_copies = to_doms(agg_out, agg_in)
+    agg_in[dom] = agg_out[dom]
+
+    grad_passed = forward(grad_far, all_grad_out)
+    agg_passed = forward(agg_far, all_agg)
+    arrived([grad_near] + grad_passed)
+    arrived(agg_copies)
+    total = dot(agg_in[0], all_grad_out[0])
+    for d in range(1, doms):
+        total = total + dot(agg_in[d], all_grad_out[d])
+    per_group = D // groups
+    for g in range(groups):
+        for n in range(0, per_group, TILE):
+            start = g * per_group + n
+            block = total[:, start : start + TILE].T
+            second_terms[g, n : n + TILE, :] = block
+            second_sent[g, n : n + TILE, :] = block.astype(BF16)
+    second_copies = to_groups(second_sent, second_in)
+
+    arrived([agg_near] + agg_passed)
+    arrived(dz_copies)
+    total = dot(dz_in[0], all_agg[0])
+    for d in range(1, doms):
+        total = total + dot(dz_in[d], all_agg[d])
+    first_terms[...] = total.reshape(first_terms.shape)
+    first_sent[...] = total.astype(BF16).reshape(first_sent.shape)
+    first_copies = to_groups(first_sent, first_in)
+
+    arrived(second_copies)
+    second_in[group] = jnp.zeros(second_in.shape[1:], BF16)
+    total = second_terms[group]
+    for g in range(groups):
+        total = total + second_in[g].astype(F32)
+    rows_out[...] = (total * factor).reshape(rows_out.shape)
+    row_copies = to_doms(rows_out, rows_in)
+    rows_in[dom] = rows_out[dom]
+
+    arrived(first_copies)
+    first_in[group] = jnp.zeros(first_in.shape[1:], BF16)
+    total = first_terms[group]
+    for g in range(groups):
+        total = total + first_in[g].astype(F32)
+    grad_first[...] = total * factor
+
+    arrived(row_copies)
+    for d in range(doms):
+        grad_second[:, d * wide : (d + 1) * wide] = rows_in[d]
+    for copy in used:
+        copy.wait_send()
+
+
+def in_kernel(
+    feats, history, grad_out, w_first, w_second, send_index, halo_index, hub_rows, tile_cols, tile_vals
+):
+    groups, doms = lax.axis_size("group"), lax.axis_size("dom")
+    share = D // (groups * doms)
+    cap, hubs = send_index.shape[2], hub_rows.shape[1]
+    wide, per_group = D // doms, D // groups
+    index_rows = jnp.concatenate(
+        [
+            send_index.reshape(1, V_DEV),
+            jnp.tile(hub_rows, (1, groups)),
+            halo_index.reshape(HALO // TILE, TILE),
+        ],
+        axis=0,
+    )
+    copies = 7 * (doms - 1) + 5 * (groups - 1)
+    vmem = pl.BlockSpec(memory_space=pltpu.VMEM)
+    hbm = pl.BlockSpec(memory_space=pl.ANY)
+    held = pltpu.VMEM
+    return pl.pallas_call(
+        functools.partial(window_kernel, groups, doms),
+        out_shape=(
+            jax.ShapeDtypeStruct((V_DEV, D), BF16),
+            jax.ShapeDtypeStruct((V_DEV, D), BF16),
+            jax.ShapeDtypeStruct((share, D), F32),
+            jax.ShapeDtypeStruct((share, D), F32),
+        ),
+        in_specs=[vmem] * 6 + [hbm] * 2,
+        out_specs=(vmem,) * 4,
+        scratch_shapes=[
+            held((D, D), BF16),
+            held((D, D), BF16),
+            held((doms, cap, D), BF16),
+            held((doms, cap, D), BF16),
+            held((hubs, D), BF16),
+            held((hubs, D), BF16),
+            held((doms, cap, D), BF16),
+            held((doms, cap, D), BF16),
+            held((groups, hubs, D), BF16),
+            held((groups, hubs, D), BF16),
+            held((doms, V_DEV, D), BF16),
+            held((doms, V_DEV, D), BF16),
+            held((groups, hubs, D), BF16),
+            held((groups, hubs, D), BF16),
+            held((V_DEV, D), F32),
+            held((V_DEV, D), F32),
+            held((doms, groups * share, V_DEV), BF16),
+            held((doms, groups * share, V_DEV), BF16),
+            held((doms, wide, V_DEV), BF16),
+            held((doms, wide, V_DEV), BF16),
+            held((groups, share, D), F32),
+            held((groups, share, D), BF16),
+            held((groups, share, D), BF16),
+            held((groups, per_group, wide), F32),
+            held((groups, per_group, wide), BF16),
+            held((groups, per_group, wide), BF16),
+            held((doms, share, wide), F32),
+            held((doms, share, wide), F32),
+            pltpu.SemaphoreType.DMA((2,)),
+            pltpu.SemaphoreType.DMA((copies,)),
+            pltpu.SemaphoreType.DMA((copies,)),
+        ],
+        compiler_params=pltpu.CompilerParams(
+            collective_id=0, has_side_effects=True, vmem_limit_bytes=48 * 1024 * 1024
+        ),
+    )(feats, history, grad_out, index_rows, tile_cols, tile_vals, w_first, w_second)
+
+
+def fits_kernel(groups, doms, cap, hubs):
+    return (
+        D % (groups * doms * 16) == 0
+        and TILE % (D // (groups * doms)) == 0
+        and D // doms == V_DEV
+        and doms * cap == V_DEV
+        and groups * hubs == V_DEV
+    )
+
+
+def window(*args):
+    send_index, hub_rows = args[5], args[7]
+    groups, doms = lax.axis_size("group"), lax.axis_size("dom")
+    if fits_kernel(groups, doms, send_index.shape[2], hub_rows.shape[1]):
+        return in_kernel(*args)
+    return on_device(*args)
+
+
 def solution(mesh):
     placed = (
         P(("group", "dom"), None),
@@ -99,7 +456,7 @@
         P(("group", "dom"), None, None, None),
     )
     return jax.shard_map(
-        on_device,
+        window,
         mesh=mesh,
         in_specs=placed,
         out_specs=(

time: 163 us -> 69.3 us (0.43)
  Pallas kernels: 0 us -> 55.2 us
  blocking collectives: 52 us -> 0 us
  waiting for transfers between devices: 32.7 us -> 0 us
  matrix products: 19.6 us -> 0 us
  between operations: 15.5 us -> 0.65 us
  local copies, waits for them, and re-layouts: 23 us -> 11.8 us
  starting transfers between devices: 9.18 us -> 0 us
  other arithmetic: 9.65 us -> 0.69 us
    pallas_call x0 -> x1, Pallas kernels: none -> 55.2 us  [in_kernel(): pl.pallas_call(functools.partial(window_kernel, groups, doms), out_shape=...]
    all_gather x2 -> x0, blocking collectives: 30.4 us -> none  [the longest x1 16.4 us: on_device(): hub_first = lax.all_gather(feats[owned_hubs], 'group', axis=0, tiled=True)]
    reduce_scatter x3 -> x0, waiting for transfers between devices: 21.8 us -> none  [the longest x2 21.8 us: reduce_weight(): summed = lax.psum_scatter(product, 'group', scatter_dimension=0, tiled=True)]
    all_to_all x2 -> x0, blocking collectives: 21.6 us -> none  [reduce_weight(): lax.all_to_all(by_dom, 'dom', split_axis=0, concat_axis=0, tiled=True)]
    dot_general x7 -> x0, matrix products: 19.6 us -> none  [the longest x2 6.44 us: reduce_weight(): lax.dot_general(columns, gathered, (((0,), (0,)), ((), ())), preferred_el...]
    gather x8 -> x0, local copies, waits for them, and re-layouts: 14 us -> none  [the longest x2 4.08 us: combine_tiles(): picked = source.reshape(-1, tile_vals.shape[2], feature_width)[tile_cols]]
    all_to_all x2 -> x0, starting transfers between devices: 8.98 us -> none  [the longest x1 5.17 us: on_device(): lax.all_to_all(feats[routes], 'dom', split_axis=0, concat_axis=0, tiled=T...]
    unnamed x31 -> x18, local copies, waits for them, and re-layouts: 2.75 us -> 10.3 us
  transfers between devices with their start and end apart: 7 -> 0, of which waited for: 4 -> 0; matrix products, arithmetic and copies ran while one was open for 22% -> 0% of each run, Pallas kernels for 0% -> 0%
where the time goes in v2:
time: 69.3 us; the launch traced here: 68.4 us
  Pallas kernels  55.2 us (80%)
  local copies, waits for them, and re-layouts  11.8 us (17%)
    pallas_call x1, Pallas kernels, in_kernel(): pl.pallas_call(functools.partial(window_kernel, groups, doms), out_shape=...  55.2 us
    unnamed x18, local copies, waits for them, and re-layouts  10.3 us

profile of v2, /device:TPU:0, one launch (start us, length us, event | category | flops | bytes accessed | tf_op | source)
XLA Modules:
  0.0 68.4 jit_solution(14029976196408465572)
XLA Ops:
  0.6 0.8 %reshape.20 = s32[1,128]{1,0:T(1,128)S(1)} reshape(s32[1,8,16]{2,1,0:T(8,128)} %param.15) | data formatting | bytes 1024 | tf_op jit(solution)/shard_map/reshape | solution.py:368
  1.4 0.7 tile.12
  2.1 0.1 tile.13
  2.1 0.7 %pad_add_fusion.index_rows = s32[6,128]{1,0:T(8,128)S(1)} fusion(s32[4,128]{1,0:T(4,128)} %bitcast.2, s32[1,128]{1,0:T(1,128)S(1)} %tile.13, s32[1,128]{1,0:T(1,128)S(1)} %reshape.20), kind=kLoop, calls=%fused_computation | loop fusion | flops 1536 | bytes 6144 | tf_op jit(solution)/shard_map/concatenate | solution.py:366
  2.8 0.0 copy-start
  2.8 1.6 %copy-done = bf16[1024,1024]{1,0:T(8,128)(2,1)S(1)} copy-done((bf16[1024,1024]{1,0:T(8,128)(2,1)S(1)}, bf16[1024,1024]{1,0:T(8,128)(2,1)}, u32[]{:S(2)}) %copy-start) | copy-done | bytes 2097176
  4.4 0.0 copy-start.1
  4.4 1.6 %copy-done.1 = bf16[1024,1024]{1,0:T(8,128)(2,1)S(1)} copy-done((bf16[1024,1024]{1,0:T(8,128)(2,1)S(1)}, bf16[1024,1024]{1,0:T(8,128)(2,1)}, u32[]{:S(2)}) %copy-start.1) | copy-done | bytes 2097176
  6.0 0.0 copy-start.2
  6.0 0.9 %copy-done.2 = bf16[128,1024]{1,0:T(8,128)(2,1)S(1)} copy-done((bf16[128,1024]{1,0:T(8,128)(2,1)S(1)}, bf16[128,1024]{1,0:T(8,128)(2,1)}, u32[]{:S(2)}) %copy-start.2) | copy-done | bytes 262168
  7.0 0.0 copy-start.3
  7.0 0.9 %copy-done.3 = bf16[128,1024]{1,0:T(8,128)(2,1)S(1)} copy-done((bf16[128,1024]{1,0:T(8,128)(2,1)S(1)}, bf16[128,1024]{1,0:T(8,128)(2,1)}, u32[]{:S(2)}) %copy-start.3) | copy-done | bytes 262168
  7.9 0.0 copy-start.4
  7.9 0.9 %copy-done.4 = bf16[128,1024]{1,0:T(8,128)(2,1)S(1)} copy-done((bf16[128,1024]{1,0:T(8,128)(2,1)S(1)}, bf16[128,1024]{1,0:T(8,128)(2,1)}, u32[]{:S(2)}) %copy-start.4) | copy-done | bytes 262168
  8.9 0.0 copy-start.5
  8.9 0.9 %copy-done.5 = bf16[1,4,128,128]{3,2,1,0:T(8,128)(2,1)S(1)} copy-done((bf16[1,4,128,128]{3,2,1,0:T(8,128)(2,1)S(1)}, bf16[1,4,128,128]{3,2,1,0:T(8,128)(2,1)}, u32[]{:S(2)}) %copy-start.5) | copy-done | bytes 131096
  9.8 0.0 copy-start.6
  9.8 0.7 copy-done.6
  10.4 55.2 %shard_map.129 = (bf16[128,1024]{1,0:T(8,128)(2,1)S(1)}, bf16[128,1024]{1,0:T(8,128)(2,1)S(1)}, f32[32,1024]{1,0:T(8,128)S(1)}, f32[32,1024]{1,0:T(8,128)S(1)}) custom-call(bf16[128,1024]{1,0:T(8,128)(2,1)S(1)} %copy-done.2, bf16[128,1024]{1,0:T(8,128)(2,1)S(1)} %copy-done.3, bf16[128,1024]{1,0:T(8,128)(2,1)S(1)} %copy-done.4, ...), custom_call_target="tpu_custom_call" | custom-call | tf_op jit(solution)/shard_map/pallas_call | solution.py:378
  65.7 0.7 %copy.18 = bf16[128,1024]{1,0:T(8,128)(2,1)} copy(bf16[128,1024]{1,0:T(8,128)(2,1)S(1)} %get-tuple-element.8) | data formatting | bytes 524288
  66.4 0.7 %copy.19 = bf16[128,1024]{1,0:T(8,128)(2,1)} copy(bf16[128,1024]{1,0:T(8,128)(2,1)S(1)} %get-tuple-element.9) | data formatting | bytes 524288
  67.1 0.7 copy.20
  67.7 0.7 copy.21
Async XLA Ops:
  2.8 1.6 %copy-start = (bf16[1024,1024]{1,0:T(8,128)(2,1)S(1)}, bf16[1024,1024]{1,0:T(8,128)(2,1)}, u32[]{:S(2)}) copy-start(bf16[1024,1024]{1,0:T(8,128)(2,1)} %w_first.1) | copy-start | bytes 6291460
  4.4 1.6 %copy-start.1 = (bf16[1024,1024]{1,0:T(8,128)(2,1)S(1)}, bf16[1024,1024]{1,0:T(8,128)(2,1)}, u32[]{:S(2)}) copy-start(bf16[1024,1024]{1,0:T(8,128)(2,1)} %w_second.1) | copy-start | bytes 6291460
  6.0 0.9 %copy-start.2 = (bf16[128,1024]{1,0:T(8,128)(2,1)S(1)}, bf16[128,1024]{1,0:T(8,128)(2,1)}, u32[]{:S(2)}) copy-start(bf16[128,1024]{1,0:T(8,128)(2,1)} %feats.1) | copy-start | bytes 786436
  7.0 0.9 %copy-start.3 = (bf16[128,1024]{1,0:T(8,128)(2,1)S(1)}, bf16[128,1024]{1,0:T(8,128)(2,1)}, u32[]{:S(2)}) copy-start(bf16[128,1024]{1,0:T(8,128)(2,1)} %history.1) | copy-start | bytes 786436
  7.9 0.9 %copy-start.4 = (bf16[128,1024]{1,0:T(8,128)(2,1)S(1)}, bf16[128,1024]{1,0:T(8,128)(2,1)}, u32[]{:S(2)}) copy-start(bf16[128,1024]{1,0:T(8,128)(2,1)} %grad_out.1) | copy-start | bytes 786436
  8.9 0.9 %copy-start.5 = (bf16[1,4,128,128]{3,2,1,0:T(8,128)(2,1)S(1)}, bf16[1,4,128,128]{3,2,1,0:T(8,128)(2,1)}, u32[]{:S(2)}) copy-start(bf16[1,4,128,128]{3,2,1,0:T(8,128)(2,1)} %tile_vals.1) | copy-start | bytes 393220
  9.8 0.7 copy-start.6

commit v3 on v2

--- a/solution.py
+++ b/solution.py
@@ -111,20 +111,29 @@
 def window_kernel(
     groups,
     doms,
-    feats,
-    history,
-    grad_out,
-    index_rows,
-    tile_cols,
-    tile_vals,
+    feats_given,
+    history_given,
+    grad_given,
     w_first,
     w_second,
+    send_given,
+    halo_given,
+    hubs_given,
+    cols_given,
+    vals_given,
     new_history,
     embed_grad,
     grad_first,
     grad_second,
     w_first_held,
     w_second_held,
+    feats,
+    history,
+    send_index,
+    halo_index,
+    hub_rows,
+    tile_cols,
+    tile_vals,
     send_feats,
     send_hist,
     send_hubs,
@@ -167,10 +176,21 @@
     chip_sources = [((chip + chips - off) % chips) * 2 + core for off in range(1, chips)]
     used = []
 
-    load_second = pltpu.make_async_copy(w_second, w_second_held, local_sems.at[0])
-    load_second.start()
-    load_first = pltpu.make_async_copy(w_first, w_first_held, local_sems.at[1])
-    load_first.start()
+    loads = []
+    for source, target in (
+        (send_given, send_index),
+        (hubs_given, hub_rows),
+        (feats_given, feats),
+        (history_given, history),
+        (grad_given, all_grad_out.at[dom]),
+        (halo_given, halo_index),
+        (cols_given, tile_cols),
+        (vals_given, tile_vals),
+        (w_second, w_second_held),
+        (w_first, w_first_held),
+    ):
+        loads.append(pltpu.make_async_copy(source, target, local_sems.at[len(loads)]))
+        loads[-1].start()
 
     barrier = pltpu.get_barrier_semaphore()
     for peer in dom_peers:
@@ -219,14 +239,26 @@
         for copy in copies:
             copy.wait_recv()
 
-    sublane = lax.broadcasted_iota(jnp.int32, (V_DEV, V_DEV), 0)
     lane_row = lax.broadcasted_iota(jnp.int32, (1, V_DEV), 1)
-    route_cols = (sublane == index_rows[0:1, :]).astype(F32)
-    hub_cols = (sublane == index_rows[1:2, :]).astype(F32)
-    route_pick = route_cols.T.astype(BF16)
-    hub_count = V_DEV // groups
-    hub_pick = hub_cols.T[:hub_count].astype(BF16)
-    hub_spread = hub_cols.astype(BF16)
+    cap, hub_count = send_index.shape[2], hub_rows.shape[1]
+    loads[0].wait()
+    routes = jnp.broadcast_to(
+        send_index[0].astype(F32)[:, None, :], (doms, cap, cap)
+    ).reshape(doms * cap, cap)
+    at_lane = lax.broadcasted_iota(jnp.int32, (doms * cap, cap), 1)
+    at_slot = lax.broadcasted_iota(jnp.int32, (doms * cap, cap), 0) % cap
+    route_column = jnp.sum(jnp.where(at_lane == at_slot, routes, 0.0), axis=1, keepdims=True)
+    route_pick = (lane_row.astype(F32) == route_column).astype(F32).astype(BF16)
+    loads[1].wait()
+    hub_square = jnp.broadcast_to(hub_rows[...].astype(F32), (hub_count, hub_count))
+    diagonal = lax.broadcasted_iota(jnp.int32, (hub_count, hub_count), 0) == (
+        lax.broadcasted_iota(jnp.int32, (hub_count, hub_count), 1)
+    )
+    hub_column = jnp.sum(jnp.where(diagonal, hub_square, 0.0), axis=1, keepdims=True)
+    hub_chosen = (lane_row.astype(F32) == hub_column).astype(F32)
+    hub_pick = hub_chosen.astype(BF16)
+    hub_spread = jnp.concatenate([hub_chosen] * groups, axis=0).T.astype(BF16)
+    loads[2].wait()
 
     send_feats[...] = dot(route_pick, feats[...]).astype(BF16).reshape(send_feats.shape)
     send_hubs[...] = dot(hub_pick, feats[...]).astype(BF16)
@@ -235,29 +267,32 @@
     hub_copies = share_to_groups(send_hubs, hubs_first)
     slots_feats[dom] = send_feats[dom]
     hubs_first[group] = send_hubs[...]
+    loads[3].wait()
     send_hist[...] = dot(route_pick, history[...]).astype(BF16).reshape(send_hist.shape)
     hist_copies = to_doms(send_hist, slots_hist)
     slots_hist[dom] = send_hist[dom]
-    grad_near, grad_far = to_chips(grad_out, all_grad_out)
-    all_grad_out[dom] = grad_out[...]
+    loads[4].wait()
+    grad_near, grad_far = to_chips(all_grad_out.at[dom], all_grad_out)
 
     places = 3 * V_DEV
     place_of = lax.broadcasted_iota(jnp.int32, (places, V_DEV), 0)
     weights = jnp.zeros((V_DEV, places), F32)
     halo_tiles = HALO // TILE
+    for load in loads[5:8]:
+        load.wait()
     for tile in range(tile_vals.shape[1]):
         column = tile_cols[0:1, tile : tile + 1]
         target = jnp.where(column == 0, lane_row, lane_row + 2 * V_DEV)
         for halo in range(halo_tiles):
-            slot = index_rows[2 + halo : 3 + halo, :] + V_DEV
+            slot = halo_index[halo * TILE : (halo + 1) * TILE].reshape(1, TILE) + V_DEV
             target = jnp.where(column == halo + 1, slot, target)
         chosen = (place_of == target).astype(F32).astype(BF16)
         weights = weights + dot(tile_vals[0, tile], chosen, (1, 1))
     own, slot, hub = (weights[:, n * V_DEV : (n + 1) * V_DEV] for n in range(3))
     own_pair, slot_pair, hub_pair = halves(own), halves(slot), halves(hub)
 
-    load_second.wait()
-    agg_grad = dot(grad_out[...], w_second_held[...], (1, 1)).astype(BF16)
+    loads[8].wait()
+    agg_grad = dot(all_grad_out[dom], w_second_held[...], (1, 1)).astype(BF16)
     hub_terms[...] = apply_halves(halves(hub.T), agg_grad).astype(BF16).reshape(hub_terms.shape)
     term_copies = to_groups(hub_terms, hub_arrived)
     hub_arrived[group] = hub_terms[group]
@@ -272,7 +307,7 @@
     all_agg[dom] = agg_first
     agg_near, agg_far = to_chips(all_agg.at[dom], all_agg)
 
-    load_first.wait()
+    loads[9].wait()
     z_first = dot(agg_first, w_first_held[...])
     gate = 1.0 / (1.0 + jnp.exp(-z_first))
     fresh = (z_first * gate).astype(BF16)
@@ -312,9 +347,8 @@
     agg_passed = forward(agg_far, all_agg)
     arrived([grad_near] + grad_passed)
     arrived(agg_copies)
-    total = dot(agg_in[0], all_grad_out[0])
-    for d in range(1, doms):
-        total = total + dot(agg_in[d], all_grad_out[d])
+    blocks = jnp.concatenate([agg_in[d] for d in range(doms)], axis=1)
+    total = dot(blocks, all_grad_out[...].reshape(doms * V_DEV, D))
     per_group = D // groups
     for g in range(groups):
         for n in range(0, per_group, TILE):
@@ -326,9 +360,8 @@
 
     arrived([agg_near] + agg_passed)
     arrived(dz_copies)
-    total = dot(dz_in[0], all_agg[0])
-    for d in range(1, doms):
-        total = total + dot(dz_in[d], all_agg[d])
+    blocks = jnp.concatenate([dz_in[d] for d in range(doms)], axis=1)
+    total = dot(blocks, all_agg[...].reshape(doms * V_DEV, D))
     first_terms[...] = total.reshape(first_terms.shape)
     first_sent[...] = total.astype(BF16).reshape(first_sent.shape)
     first_copies = to_groups(first_sent, first_in)
@@ -356,6 +389,15 @@
         copy.wait_send()
 
 
+def write_kernel(*refs):
+    sems = refs[8]
+    copies = [pltpu.make_async_copy(refs[n], refs[n + 4], sems.at[n]) for n in range(4)]
+    for copy in copies:
+        copy.start()
+    for copy in copies:
+        copy.wait()
+
+
 def in_kernel(
     feats, history, grad_out, w_first, w_second, send_index, halo_index, hub_rows, tile_cols, tile_vals
 ):
@@ -363,19 +405,11 @@
     share = D // (groups * doms)
     cap, hubs = send_index.shape[2], hub_rows.shape[1]
     wide, per_group = D // doms, D // groups
-    index_rows = jnp.concatenate(
-        [
-            send_index.reshape(1, V_DEV),
-            jnp.tile(hub_rows, (1, groups)),
-            halo_index.reshape(HALO // TILE, TILE),
-        ],
-        axis=0,
-    )
     copies = 7 * (doms - 1) + 5 * (groups - 1)
     vmem = pl.BlockSpec(memory_space=pltpu.VMEM)
-    hbm = pl.BlockSpec(memory_space=pl.ANY)
+    hbm = pl.BlockSpec(memory_space=pltpu.HBM)
     held = pltpu.VMEM
-    return pl.pallas_call(
+    results = pl.pallas_call(
         functools.partial(window_kernel, groups, doms),
         out_shape=(
             jax.ShapeDtypeStruct((V_DEV, D), BF16),
@@ -383,11 +417,18 @@
             jax.ShapeDtypeStruct((share, D), F32),
             jax.ShapeDtypeStruct((share, D), F32),
         ),
-        in_specs=[vmem] * 6 + [hbm] * 2,
+        in_specs=[hbm] * 10,
         out_specs=(vmem,) * 4,
         scratch_shapes=[
             held((D, D), BF16),
             held((D, D), BF16),
+            held((V_DEV, D), BF16),
+            held((V_DEV, D), BF16),
+            held(send_index.shape, jnp.int32),
+            held(halo_index.shape, jnp.int32),
+            held(hub_rows.shape, jnp.int32),
+            held(tile_cols.shape, jnp.int32),
+            held(tile_vals.shape, BF16),
             held((doms, cap, D), BF16),
             held((doms, cap, D), BF16),
             held((hubs, D), BF16),
@@ -414,14 +455,32 @@
             held((groups, per_group, wide), BF16),
             held((doms, share, wide), F32),
             held((doms, share, wide), F32),
-            pltpu.SemaphoreType.DMA((2,)),
+            pltpu.SemaphoreType.DMA((10,)),
             pltpu.SemaphoreType.DMA((copies,)),
             pltpu.SemaphoreType.DMA((copies,)),
         ],
         compiler_params=pltpu.CompilerParams(
-            collective_id=0, has_side_effects=True, vmem_limit_bytes=48 * 1024 * 1024
+            collective_id=0, has_side_effects=True, vmem_limit_bytes=62 * 1024 * 1024
         ),
-    )(feats, history, grad_out, index_rows, tile_cols, tile_vals, w_first, w_second)
+    )(
+        feats,
+        history,
+        grad_out,
+        w_first,
+        w_second,
+        send_index,
+        halo_index,
+        hub_rows,
+        tile_cols,
+        tile_vals,
+    )
+    return pl.pallas_call(
+        write_kernel,
+        out_shape=tuple(jax.ShapeDtypeStruct(part.shape, part.dtype) for part in results),
+        in_specs=[pl.BlockSpec(memory_space=pl.ANY)] * 4,
+        out_specs=(hbm,) * 4,
+        scratch_shapes=[pltpu.SemaphoreType.DMA((4,))],
+    )(*results)
 
 
 def fits_kernel(groups, doms, cap, hubs):

time: 69.3 us -> 82 us (1.18)
  Pallas kernels: 55.2 us -> 80.7 us
  local copies, waits for them, and re-layouts: 11.8 us -> 0 us
    pallas_call x0 -> x1, Pallas kernels: none -> 25 us  [in_kernel(): pl.pallas_call(write_kernel, out_shape=tuple((jax.ShapeDtypeStruct(part.s...]
    unnamed x18 -> x0, local copies, waits for them, and re-layouts: 10.3 us -> none
where the time goes in v3:
time: 82 us; the launch traced here: 81.3 us
  Pallas kernels  80.7 us (98%)
    pallas_call x1, Pallas kernels, in_kernel(): pl.pallas_call(functools.partial(window_kernel, groups, doms), out_shape=...  55.7 us
    pallas_call x1, Pallas kernels, in_kernel(): pl.pallas_call(write_kernel, out_shape=tuple((jax.ShapeDtypeStruct(part.s...  25 us

profile of v3, /device:TPU:0, one launch (start us, length us, event | category | flops | bytes accessed | tf_op | source)
XLA Modules:
  0.0 81.3 jit_solution(11705987405846468079)
XLA Ops:
  0.6 55.7 %shard_map.129 = (bf16[128,1024]{1,0:T(8,128)(2,1)}, bf16[128,1024]{1,0:T(8,128)(2,1)}, f32[32,1024]{1,0:T(8,128)}, f32[32,1024]{1,0:T(8,128)}) custom-call(bf16[128,1024]{1,0:T(8,128)(2,1)} %feats_given.1, bf16[128,1024]{1,0:T(8,128)(2,1)} %history_given.1, bf16[128,1024]{1,0:T(8,128)(2,1)} %grad_given.1, bf16[1024,1024]{1,0:T(8,128)(2,1)} %w_first.1, ...), custom_call_target="tpu_custom_call" | custom-call | tf_op jit(solution)/shard_map/pallas_call | solution.py:412
  56.3 25.0 %shard_map.130 = (bf16[128,1024]{1,0:T(8,128)(2,1)}, bf16[128,1024]{1,0:T(8,128)(2,1)}, f32[32,1024]{1,0:T(8,128)}, f32[32,1024]{1,0:T(8,128)}) custom-call(bf16[128,1024]{1,0:T(8,128)(2,1)} %get-tuple-element.8.refs_0_, bf16[128,1024]{1,0:T(8,128)(2,1)} %get-tuple-element.9.refs_1_, f32[32,1024]{1,0:T(8,128)} %get-tuple-element.10.refs_2_, ...), custom_call_target="tpu_custom_call" | custom-call | tf_op jit(solution)/shard_map/pallas_call | solution.py:477

commit v4 on v3

--- a/solution.py
+++ b/solution.py
@@ -165,15 +165,15 @@
     recv_sems,
 ):
     group, dom = lax.axis_index("group"), lax.axis_index("dom")
-    chips = doms // 2
     chip, core = dom // 2, dom % 2
     factor = 1.0 / math.sqrt(V_DEV * groups * doms)
     share = D // (groups * doms)
     dom_peers = [(dom + off) % doms for off in range(1, doms)]
     group_peers = [(group + off) % groups for off in range(1, groups)]
     sibling = dom + 1 - 2 * core
-    chip_peers = [((chip + off) % chips) * 2 + core for off in range(1, chips)]
-    chip_sources = [((chip + chips - off) % chips) * 2 + core for off in range(1, chips)]
+    beside = (chip + 1 - 2 * (chip % 2)) * 2 + core
+    across = ((chip + 2) % 4) * 2 + core
+    opposite = (3 - chip) * 2 + core
     used = []
 
     loads = []
@@ -224,16 +224,27 @@
     def share_to_groups(source, target):
         return [send(source, target.at[group], peer, dom) for peer in group_peers]
 
-    def to_chips(source, target):
-        near = send(source, target.at[dom], group, sibling)
-        return near, [send(source, target.at[dom], group, peer) for peer in chip_peers]
-
-    def forward(far, target):
-        passed = []
-        for copy, origin in zip(far, chip_sources):
-            copy.wait_recv()
-            passed.append(send(target.at[origin], target.at[origin], group, sibling))
-        return passed
+    def to_near(target):
+        block = target.at[dom]
+        return [send(block, block, group, peer) for peer in (sibling, beside, across)]
+
+    def relay(near, target):
+        near[1].wait_recv()
+        block = target.at[beside]
+        upper = target.at[beside, pl.ds(0, V_DEV // 2)]
+        parts = [send(upper, upper, group, across)]
+        passed = [send(block, block, group, sibling)]
+        near[2].wait_recv()
+        block = target.at[across]
+        lower = target.at[across, pl.ds(V_DEV // 2, V_DEV // 2)]
+        parts.append(send(lower, lower, group, beside))
+        passed.append(send(block, block, group, sibling))
+        return parts, passed
+
+    def finish(near, parts, passed, target):
+        arrived(parts)
+        block = target.at[opposite]
+        arrived([near[0]] + passed + [send(block, block, group, sibling)])
 
     def arrived(copies):
         for copy in copies:
@@ -272,7 +283,7 @@
     hist_copies = to_doms(send_hist, slots_hist)
     slots_hist[dom] = send_hist[dom]
     loads[4].wait()
-    grad_near, grad_far = to_chips(all_grad_out.at[dom], all_grad_out)
+    grad_near = to_near(all_grad_out)
 
     places = 3 * V_DEV
     place_of = lax.broadcasted_iota(jnp.int32, (places, V_DEV), 0)
@@ -305,7 +316,7 @@
     first = first + apply_halves(hub_pair, hubs_first[...].reshape(V_DEV, D))
     agg_first = first.astype(BF16)
     all_agg[dom] = agg_first
-    agg_near, agg_far = to_chips(all_agg.at[dom], all_agg)
+    agg_near = to_near(all_agg)
 
     loads[9].wait()
     z_first = dot(agg_first, w_first_held[...])
@@ -331,6 +342,7 @@
                 ]
     dz_copies = to_doms(dz_out, dz_in)
     dz_in[dom] = dz_out[dom]
+    grad_parts, grad_passed = relay(grad_near, all_grad_out)
 
     arrived(hist_copies)
     second = apply_halves(own_pair, new_history[...])
@@ -343,9 +355,8 @@
     agg_copies = to_doms(agg_out, agg_in)
     agg_in[dom] = agg_out[dom]
 
-    grad_passed = forward(grad_far, all_grad_out)
-    agg_passed = forward(agg_far, all_agg)
-    arrived([grad_near] + grad_passed)
+    finish(grad_near, grad_parts, grad_passed, all_grad_out)
+    agg_parts, agg_passed = relay(agg_near, all_agg)
     arrived(agg_copies)
     blocks = jnp.concatenate([agg_in[d] for d in range(doms)], axis=1)
     total = dot(blocks, all_grad_out[...].reshape(doms * V_DEV, D))
@@ -358,7 +369,7 @@
             second_sent[g, n : n + TILE, :] = block.astype(BF16)
     second_copies = to_groups(second_sent, second_in)
 
-    arrived([agg_near] + agg_passed)
+    finish(agg_near, agg_parts, agg_passed, all_agg)
     arrived(dz_copies)
     blocks = jnp.concatenate([dz_in[d] for d in range(doms)], axis=1)
     total = dot(blocks, all_agg[...].reshape(doms * V_DEV, D))
@@ -389,15 +400,6 @@
         copy.wait_send()
 
 
-def write_kernel(*refs):
-    sems = refs[8]
-    copies = [pltpu.make_async_copy(refs[n], refs[n + 4], sems.at[n]) for n in range(4)]
-    for copy in copies:
-        copy.start()
-    for copy in copies:
-        copy.wait()
-
-
 def in_kernel(
     feats, history, grad_out, w_first, w_second, send_index, halo_index, hub_rows, tile_cols, tile_vals
 ):
@@ -405,11 +407,11 @@
     share = D // (groups * doms)
     cap, hubs = send_index.shape[2], hub_rows.shape[1]
     wide, per_group = D // doms, D // groups
-    copies = 7 * (doms - 1) + 5 * (groups - 1)
+    copies = 5 * (doms - 1) + 5 * (groups - 1) + 16
     vmem = pl.BlockSpec(memory_space=pltpu.VMEM)
     hbm = pl.BlockSpec(memory_space=pltpu.HBM)
     held = pltpu.VMEM
-    results = pl.pallas_call(
+    return pl.pallas_call(
         functools.partial(window_kernel, groups, doms),
         out_shape=(
             jax.ShapeDtypeStruct((V_DEV, D), BF16),
@@ -460,7 +462,7 @@
             pltpu.SemaphoreType.DMA((copies,)),
         ],
         compiler_params=pltpu.CompilerParams(
-            collective_id=0, has_side_effects=True, vmem_limit_bytes=62 * 1024 * 1024
+            collective_id=0, has_side_effects=True, vmem_limit_bytes=60 * 1024 * 1024
         ),
     )(
         feats,
@@ -474,19 +476,13 @@
         tile_cols,
         tile_vals,
     )
-    return pl.pallas_call(
-        write_kernel,
-        out_shape=tuple(jax.ShapeDtypeStruct(part.shape, part.dtype) for part in results),
-        in_specs=[pl.BlockSpec(memory_space=pl.ANY)] * 4,
-        out_specs=(hbm,) * 4,
-        scratch_shapes=[pltpu.SemaphoreType.DMA((4,))],
-    )(*results)
 
 
 def fits_kernel(groups, doms, cap, hubs):
     return (
         D % (groups * doms * 16) == 0
         and TILE % (D // (groups * doms)) == 0
+        and doms == 8
         and D // doms == V_DEV
         and doms * cap == V_DEV
         and groups * hubs == V_DEV

time: 82 us -> 54.8 us (0.67)
  Pallas kernels: 80.7 us -> 47.5 us
  local copies, waits for them, and re-layouts: 0 us -> 6.47 us
    pallas_call x1 -> x0, Pallas kernels: 25 us -> none  [in_kernel(): pl.pallas_call(write_kernel, out_shape=tuple((jax.ShapeDtypeStruct(part.s...]
    pallas_call x1, Pallas kernels: 55.7 us -> 47.5 us  [in_kernel(): pl.pallas_call(functools.partial(window_kernel, groups, doms), out_shape=...]
    unnamed x0 -> x4, local copies, waits for them, and re-layouts: none -> 6.47 us
where the time goes in v4:
time: 54.8 us; the launch traced here: 54.6 us
  Pallas kernels  47.5 us (87%)
  local copies, waits for them, and re-layouts  6.47 us (12%)
  between operations  0.64 us (1%)
    pallas_call x1, Pallas kernels, in_kernel(): pl.pallas_call(functools.partial(window_kernel, groups, doms), out_shape=...  47.5 us
    unnamed x4, local copies, waits for them, and re-layouts  6.47 us

profile of v4, /device:TPU:0, one launch (start us, length us, event | category | flops | bytes accessed | tf_op | source)
XLA Modules:
  0.0 54.6 jit_solution(3585548319697287691)
XLA Ops:
  0.6 47.5 %shard_map.129 = (bf16[128,1024]{1,0:T(8,128)(2,1)}, bf16[128,1024]{1,0:T(8,128)(2,1)}, f32[32,1024]{1,0:T(8,128)}, f32[32,1024]{1,0:T(8,128)}) custom-call(bf16[128,1024]{1,0:T(8,128)(2,1)} %feats_given.1, bf16[128,1024]{1,0:T(8,128)(2,1)} %history_given.1, bf16[128,1024]{1,0:T(8,128)(2,1)} %grad_given.1, bf16[1024,1024]{1,0:T(8,128)(2,1)} %w_first.1, ...), custom_call_target="tpu_custom_call" | custom-call | tf_op jit(solution)/shard_map/pallas_call | solution.py:414
  48.1 1.7 %copy.18 = bf16[128,1024]{1,0:T(8,128)(2,1)} copy(bf16[128,1024]{1,0:T(8,128)(2,1)} %get-tuple-element.8) | data formatting | bytes 524288
  49.8 1.7 %copy.19 = bf16[128,1024]{1,0:T(8,128)(2,1)} copy(bf16[128,1024]{1,0:T(8,128)(2,1)} %get-tuple-element.9) | data formatting | bytes 524288
  51.5 1.6 %copy.20 = f32[32,1024]{1,0:T(8,128)} copy(f32[32,1024]{1,0:T(8,128)} %get-tuple-element.10) | data formatting | bytes 262144
  53.1 1.6 %copy.21 = f32[32,1024]{1,0:T(8,128)} copy(f32[32,1024]{1,0:T(8,128)} %get-tuple-element.11) | data formatting | bytes 262144

commit v5 on v4

--- a/solution.py
+++ b/solution.py
@@ -176,6 +176,16 @@
     opposite = (3 - chip) * 2 + core
     used = []
 
+    barrier = pltpu.get_barrier_semaphore()
+    for peer in dom_peers:
+        pl.semaphore_signal(
+            barrier, inc=1, device_id=(group, peer), device_id_type=pl.DeviceIdType.MESH
+        )
+    for peer in group_peers:
+        pl.semaphore_signal(
+            barrier, inc=1, device_id=(peer, dom), device_id_type=pl.DeviceIdType.MESH
+        )
+
     loads = []
     for source, target in (
         (send_given, send_index),
@@ -192,16 +202,6 @@
         loads.append(pltpu.make_async_copy(source, target, local_sems.at[len(loads)]))
         loads[-1].start()
 
-    barrier = pltpu.get_barrier_semaphore()
-    for peer in dom_peers:
-        pl.semaphore_signal(
-            barrier, inc=1, device_id=(group, peer), device_id_type=pl.DeviceIdType.MESH
-        )
-    for peer in group_peers:
-        pl.semaphore_signal(
-            barrier, inc=1, device_id=(peer, dom), device_id_type=pl.DeviceIdType.MESH
-        )
-
     def send(source, target, to_group, to_dom):
         copy = pltpu.make_async_remote_copy(
             src_ref=source,
@@ -271,19 +271,17 @@
     hub_spread = jnp.concatenate([hub_chosen] * groups, axis=0).T.astype(BF16)
     loads[2].wait()
 
-    send_feats[...] = dot(route_pick, feats[...]).astype(BF16).reshape(send_feats.shape)
     send_hubs[...] = dot(hub_pick, feats[...]).astype(BF16)
     pl.semaphore_wait(barrier, doms - 1 + groups - 1)
+    hub_copies = share_to_groups(send_hubs, hubs_first)
+    send_feats[...] = dot(route_pick, feats[...]).astype(BF16).reshape(send_feats.shape)
     feat_copies = to_doms(send_feats, slots_feats)
-    hub_copies = share_to_groups(send_hubs, hubs_first)
     slots_feats[dom] = send_feats[dom]
     hubs_first[group] = send_hubs[...]
     loads[3].wait()
     send_hist[...] = dot(route_pick, history[...]).astype(BF16).reshape(send_hist.shape)
-    hist_copies = to_doms(send_hist, slots_hist)
     slots_hist[dom] = send_hist[dom]
     loads[4].wait()
-    grad_near = to_near(all_grad_out)
 
     places = 3 * V_DEV
     place_of = lax.broadcasted_iota(jnp.int32, (places, V_DEV), 0)
@@ -305,14 +303,16 @@
     loads[8].wait()
     agg_grad = dot(all_grad_out[dom], w_second_held[...], (1, 1)).astype(BF16)
     hub_terms[...] = apply_halves(halves(hub.T), agg_grad).astype(BF16).reshape(hub_terms.shape)
-    term_copies = to_groups(hub_terms, hub_arrived)
     hub_arrived[group] = hub_terms[group]
     own_grad[...] = apply_halves(halves(own.T), agg_grad)
 
     first = apply_halves(own_pair, feats[...])
     arrived(feat_copies)
+    grad_near = to_near(all_grad_out)
+    hist_copies = to_doms(send_hist, slots_hist)
     first = first + apply_halves(slot_pair, slots_feats[...].reshape(V_DEV, D))
     arrived(hub_copies)
+    term_copies = to_groups(hub_terms, hub_arrived)
     first = first + apply_halves(hub_pair, hubs_first[...].reshape(V_DEV, D))
     agg_first = first.astype(BF16)
     all_agg[dom] = agg_first
@@ -400,6 +400,19 @@
         copy.wait_send()
 
 
+def write_kernel(*refs):
+    given, written, staged, sems = refs[:4], refs[4:8], refs[8:12], refs[12]
+    reads = [pltpu.make_async_copy(given[n], staged[n], sems.at[n]) for n in range(4)]
+    writes = [pltpu.make_async_copy(staged[n], written[n], sems.at[n + 4]) for n in range(4)]
+    for copy in reads:
+        copy.start()
+    for read, write in zip(reads, writes):
+        read.wait()
+        write.start()
+    for copy in writes:
+        copy.wait()
+
+
 def in_kernel(
     feats, history, grad_out, w_first, w_second, send_index, halo_index, hub_rows, tile_cols, tile_vals
 ):
@@ -411,7 +424,7 @@
     vmem = pl.BlockSpec(memory_space=pltpu.VMEM)
     hbm = pl.BlockSpec(memory_space=pltpu.HBM)
     held = pltpu.VMEM
-    return pl.pallas_call(
+    results = pl.pallas_call(
         functools.partial(window_kernel, groups, doms),
         out_shape=(
             jax.ShapeDtypeStruct((V_DEV, D), BF16),
@@ -476,6 +489,15 @@
         tile_cols,
         tile_vals,
     )
+    shapes = [(part.shape, part.dtype) for part in results]
+    return pl.pallas_call(
+        write_kernel,
+        out_shape=tuple(jax.ShapeDtypeStruct(*shape) for shape in shapes),
+        in_specs=[pl.BlockSpec(memory_space=pl.ANY)] * 4,
+        out_specs=(hbm,) * 4,
+        scratch_shapes=[held(*shape) for shape in shapes] + [pltpu.SemaphoreType.DMA((8,))],
+        compiler_params=pltpu.CompilerParams(vmem_limit_bytes=60 * 1024 * 1024),
+    )(*results)
 
 
 def fits_kernel(groups, doms, cap, hubs):

time: 54.8 us -> 52.7 us (0.962)
  local copies, waits for them, and re-layouts: 6.47 us -> 0 us
  Pallas kernels: 47.5 us -> 51.8 us
    unnamed x4 -> x0, local copies, waits for them, and re-layouts: 6.47 us -> none
    pallas_call x1, Pallas kernels: 47.5 us -> 49.9 us  [in_kernel(): pl.pallas_call(functools.partial(window_kernel, groups, doms), out_shape=...]
    pallas_call x0 -> x1, Pallas kernels: none -> 1.89 us  [in_kernel(): pl.pallas_call(write_kernel, out_shape=tuple((jax.ShapeDtypeStruct(*shape...]
where the time goes in v5:
time: 52.7 us; the launch traced here: 52.5 us
  Pallas kernels  51.8 us (98%)
  between operations  0.64 us (1%)
    pallas_call x1, Pallas kernels, in_kernel(): pl.pallas_call(functools.partial(window_kernel, groups, doms), out_shape=...  49.9 us
    pallas_call x1, Pallas kernels, in_kernel(): pl.pallas_call(write_kernel, out_shape=tuple((jax.ShapeDtypeStruct(*shape...  1.89 us

profile of v5, /device:TPU:0, one launch (start us, length us, event | category | flops | bytes accessed | tf_op | source)
XLA Modules:
  0.0 52.5 jit_solution(13198308413902536923)
XLA Ops:
  0.6 49.9 %shard_map.129 = (bf16[128,1024]{1,0:T(8,128)(2,1)}, bf16[128,1024]{1,0:T(8,128)(2,1)}, f32[32,1024]{1,0:T(8,128)}, f32[32,1024]{1,0:T(8,128)}) custom-call(bf16[128,1024]{1,0:T(8,128)(2,1)} %feats_given.1, bf16[128,1024]{1,0:T(8,128)(2,1)} %history_given.1, bf16[128,1024]{1,0:T(8,128)(2,1)} %grad_given.1, bf16[1024,1024]{1,0:T(8,128)(2,1)} %w_first.1, ...), custom_call_target="tpu_custom_call" | custom-call | tf_op jit(solution)/shard_map/pallas_call | solution.py:427
  50.6 1.9 %shard_map.130 = (bf16[128,1024]{1,0:T(8,128)(2,1)}, bf16[128,1024]{1,0:T(8,128)(2,1)}, f32[32,1024]{1,0:T(8,128)}, f32[32,1024]{1,0:T(8,128)}) custom-call(bf16[128,1024]{1,0:T(8,128)(2,1)} %get-tuple-element.8.refs_0_, bf16[128,1024]{1,0:T(8,128)(2,1)} %get-tuple-element.9.refs_1_, f32[32,1024]{1,0:T(8,128)} %get-tuple-element.10.refs_2_, ...), custom_call_target="tpu_custom_call" | custom-call | tf_op jit(solution)/shard_map/pallas_call | solution.py:493

commit v6 on v5

--- a/solution.py
+++ b/solution.py
@@ -276,12 +276,14 @@
     hub_copies = share_to_groups(send_hubs, hubs_first)
     send_feats[...] = dot(route_pick, feats[...]).astype(BF16).reshape(send_feats.shape)
     feat_copies = to_doms(send_feats, slots_feats)
+    loads[4].wait()
+    grad_near = to_near(all_grad_out)
     slots_feats[dom] = send_feats[dom]
     hubs_first[group] = send_hubs[...]
     loads[3].wait()
     send_hist[...] = dot(route_pick, history[...]).astype(BF16).reshape(send_hist.shape)
+    hist_copies = to_doms(send_hist, slots_hist)
     slots_hist[dom] = send_hist[dom]
-    loads[4].wait()
 
     places = 3 * V_DEV
     place_of = lax.broadcasted_iota(jnp.int32, (places, V_DEV), 0)
@@ -303,16 +305,14 @@
     loads[8].wait()
     agg_grad = dot(all_grad_out[dom], w_second_held[...], (1, 1)).astype(BF16)
     hub_terms[...] = apply_halves(halves(hub.T), agg_grad).astype(BF16).reshape(hub_terms.shape)
+    term_copies = to_groups(hub_terms, hub_arrived)
     hub_arrived[group] = hub_terms[group]
     own_grad[...] = apply_halves(halves(own.T), agg_grad)
 
     first = apply_halves(own_pair, feats[...])
     arrived(feat_copies)
-    grad_near = to_near(all_grad_out)
-    hist_copies = to_doms(send_hist, slots_hist)
     first = first + apply_halves(slot_pair, slots_feats[...].reshape(V_DEV, D))
     arrived(hub_copies)
-    term_copies = to_groups(hub_terms, hub_arrived)
     first = first + apply_halves(hub_pair, hubs_first[...].reshape(V_DEV, D))
     agg_first = first.astype(BF16)
     all_agg[dom] = agg_first

time: 52.7 us -> 50.5 us (0.958)
  Pallas kernels: 51.8 us -> 49.7 us
    pallas_call x1, Pallas kernels: 49.9 us -> 47.8 us  [in_kernel(): pl.pallas_call(functools.partial(window_kernel, groups, doms), out_shape=...]
where the time goes in v6:
time: 50.5 us; the launch traced here: 50.3 us
  Pallas kernels  49.7 us (98%)
  between operations  0.64 us (1%)
    pallas_call x1, Pallas kernels, in_kernel(): pl.pallas_call(functools.partial(window_kernel, groups, doms), out_shape=...  47.8 us
    pallas_call x1, Pallas kernels, in_kernel(): pl.pallas_call(write_kernel, out_shape=tuple((jax.ShapeDtypeStruct(*shape...  1.89 us

profile of v6, /device:TPU:0, one launch (start us, length us, event | category | flops | bytes accessed | tf_op | source)
XLA Modules:
  0.0 50.3 jit_solution(6896557377129323475)
XLA Ops:
  0.6 47.8 %shard_map.129 = (bf16[128,1024]{1,0:T(8,128)(2,1)}, bf16[128,1024]{1,0:T(8,128)(2,1)}, f32[32,1024]{1,0:T(8,128)}, f32[32,1024]{1,0:T(8,128)}) custom-call(bf16[128,1024]{1,0:T(8,128)(2,1)} %feats_given.1, bf16[128,1024]{1,0:T(8,128)(2,1)} %history_given.1, bf16[128,1024]{1,0:T(8,128)(2,1)} %grad_given.1, bf16[1024,1024]{1,0:T(8,128)(2,1)} %w_first.1, ...), custom_call_target="tpu_custom_call" | custom-call | tf_op jit(solution)/shard_map/pallas_call | solution.py:427
  48.4 1.9 %shard_map.130 = (bf16[128,1024]{1,0:T(8,128)(2,1)}, bf16[128,1024]{1,0:T(8,128)(2,1)}, f32[32,1024]{1,0:T(8,128)}, f32[32,1024]{1,0:T(8,128)}) custom-call(bf16[128,1024]{1,0:T(8,128)(2,1)} %get-tuple-element.8.refs_0_, bf16[128,1024]{1,0:T(8,128)(2,1)} %get-tuple-element.9.refs_1_, f32[32,1024]{1,0:T(8,128)} %get-tuple-element.10.refs_2_, ...), custom_call_target="tpu_custom_call" | custom-call | tf_op jit(solution)/shard_map/pallas_call | solution.py:493

commit v7 on v6

--- a/solution.py
+++ b/solution.py
@@ -327,6 +327,7 @@
     fresh_copies = share_to_groups(send_fresh, hubs_second)
     hubs_second[group] = send_fresh[...]
     gate_slope[...] = gate * (1.0 + z_first * (1.0 - gate))
+    grad_parts, grad_passed = relay(grad_near, all_grad_out)
 
     arrived(term_copies)
     vertex_grad = own_grad[...] + dot(hub_spread, hub_arrived[...].reshape(V_DEV, D))
@@ -342,11 +343,11 @@
                 ]
     dz_copies = to_doms(dz_out, dz_in)
     dz_in[dom] = dz_out[dom]
-    grad_parts, grad_passed = relay(grad_near, all_grad_out)
 
     arrived(hist_copies)
     second = apply_halves(own_pair, new_history[...])
     second = second + apply_halves(slot_pair, slots_hist[...].reshape(V_DEV, D))
+    agg_parts, agg_passed = relay(agg_near, all_agg)
     arrived(fresh_copies)
     second = second + apply_halves(hub_pair, hubs_second[...].reshape(V_DEV, D))
     wide = D // doms
@@ -356,7 +357,6 @@
     agg_in[dom] = agg_out[dom]
 
     finish(grad_near, grad_parts, grad_passed, all_grad_out)
-    agg_parts, agg_passed = relay(agg_near, all_agg)
     arrived(agg_copies)
     blocks = jnp.concatenate([agg_in[d] for d in range(doms)], axis=1)
     total = dot(blocks, all_grad_out[...].reshape(doms * V_DEV, D))

time: 50.5 us -> 53.5 us (1.059)
  Pallas kernels: 49.7 us -> 52.2 us
    pallas_call x1, Pallas kernels: 47.8 us -> 50.3 us  [in_kernel(): pl.pallas_call(functools.partial(window_kernel, groups, doms), out_shape=...]
where the time goes in v7:
time: 53.5 us; the launch traced here: 52.8 us
  Pallas kernels  52.2 us (98%)
  between operations  0.64 us (1%)
    pallas_call x1, Pallas kernels, in_kernel(): pl.pallas_call(functools.partial(window_kernel, groups, doms), out_shape=...  50.3 us
    pallas_call x1, Pallas kernels, in_kernel(): pl.pallas_call(write_kernel, out_shape=tuple((jax.ShapeDtypeStruct(*shape...  1.89 us

profile of v7, /device:TPU:0, one launch (start us, length us, event | category | flops | bytes accessed | tf_op | source)
XLA Modules:
  0.0 52.8 jit_solution(514540427185898938)
XLA Ops:
  0.6 50.3 %shard_map.129 = (bf16[128,1024]{1,0:T(8,128)(2,1)}, bf16[128,1024]{1,0:T(8,128)(2,1)}, f32[32,1024]{1,0:T(8,128)}, f32[32,1024]{1,0:T(8,128)}) custom-call(bf16[128,1024]{1,0:T(8,128)(2,1)} %feats_given.1, bf16[128,1024]{1,0:T(8,128)(2,1)} %history_given.1, bf16[128,1024]{1,0:T(8,128)(2,1)} %grad_given.1, bf16[1024,1024]{1,0:T(8,128)(2,1)} %w_first.1, ...), custom_call_target="tpu_custom_call" | custom-call | tf_op jit(solution)/shard_map/pallas_call | solution.py:427
  50.9 1.9 %shard_map.130 = (bf16[128,1024]{1,0:T(8,128)(2,1)}, bf16[128,1024]{1,0:T(8,128)(2,1)}, f32[32,1024]{1,0:T(8,128)}, f32[32,1024]{1,0:T(8,128)}) custom-call(bf16[128,1024]{1,0:T(8,128)(2,1)} %get-tuple-element.8.refs_0_, bf16[128,1024]{1,0:T(8,128)(2,1)} %get-tuple-element.9.refs_1_, f32[32,1024]{1,0:T(8,128)} %get-tuple-element.10.refs_2_, ...), custom_call_target="tpu_custom_call" | custom-call | tf_op jit(solution)/shard_map/pallas_call | solution.py:493

commit v8 on v6

--- a/solution.py
+++ b/solution.py
@@ -356,7 +356,6 @@
     agg_in[dom] = agg_out[dom]
 
     finish(grad_near, grad_parts, grad_passed, all_grad_out)
-    agg_parts, agg_passed = relay(agg_near, all_agg)
     arrived(agg_copies)
     blocks = jnp.concatenate([agg_in[d] for d in range(doms)], axis=1)
     total = dot(blocks, all_grad_out[...].reshape(doms * V_DEV, D))
@@ -368,6 +367,7 @@
             second_terms[g, n : n + TILE, :] = block
             second_sent[g, n : n + TILE, :] = block.astype(BF16)
     second_copies = to_groups(second_sent, second_in)
+    agg_parts, agg_passed = relay(agg_near, all_agg)
 
     finish(agg_near, agg_parts, agg_passed, all_agg)
     arrived(dz_copies)

time: 50.5 us -> 51.3 us (1.016)
  Pallas kernels: 49.7 us -> 50.4 us
    pallas_call x1, Pallas kernels: 47.8 us -> 48.5 us  [in_kernel(): pl.pallas_call(functools.partial(window_kernel, groups, doms), out_shape=...]
where the time goes in v8:
time: 51.3 us; the launch traced here: 51.1 us
  Pallas kernels  50.4 us (98%)
  between operations  0.64 us (1%)
    pallas_call x1, Pallas kernels, in_kernel(): pl.pallas_call(functools.partial(window_kernel, groups, doms), out_shape=...  48.5 us
    pallas_call x1, Pallas kernels, in_kernel(): pl.pallas_call(write_kernel, out_shape=tuple((jax.ShapeDtypeStruct(*shape...  1.89 us

profile of v8, /device:TPU:0, one launch (start us, length us, event | category | flops | bytes accessed | tf_op | source)
XLA Modules:
  0.0 51.1 jit_solution(15868295742368858466)
XLA Ops:
  0.6 48.5 %shard_map.129 = (bf16[128,1024]{1,0:T(8,128)(2,1)}, bf16[128,1024]{1,0:T(8,128)(2,1)}, f32[32,1024]{1,0:T(8,128)}, f32[32,1024]{1,0:T(8,128)}) custom-call(bf16[128,1024]{1,0:T(8,128)(2,1)} %feats_given.1, bf16[128,1024]{1,0:T(8,128)(2,1)} %history_given.1, bf16[128,1024]{1,0:T(8,128)(2,1)} %grad_given.1, bf16[1024,1024]{1,0:T(8,128)(2,1)} %w_first.1, ...), custom_call_target="tpu_custom_call" | custom-call | tf_op jit(solution)/shard_map/pallas_call | solution.py:427
  49.2 1.9 %shard_map.130 = (bf16[128,1024]{1,0:T(8,128)(2,1)}, bf16[128,1024]{1,0:T(8,128)(2,1)}, f32[32,1024]{1,0:T(8,128)}, f32[32,1024]{1,0:T(8,128)}) custom-call(bf16[128,1024]{1,0:T(8,128)(2,1)} %get-tuple-element.8.refs_0_, bf16[128,1024]{1,0:T(8,128)(2,1)} %get-tuple-element.9.refs_1_, f32[32,1024]{1,0:T(8,128)} %get-tuple-element.10.refs_2_, ...), custom_call_target="tpu_custom_call" | custom-call | tf_op jit(solution)/shard_map/pallas_call | solution.py:493
